TPU v7x, 1024 devices: a whole 8x8x8 slice. The times are simulated.
1024 devices in a mesh: expert: 16 (over z, x_hi), dp: 64 (over x_lo, y, core).
Axes of the slice: x: 8 (x_hi: 2, x_lo: 4; x = x_hi * 4 + x_lo), y: 8, z: 8, core: 2. Of those that a mesh axis runs over, the one named last changes fastest.
Arguments:
- grad_out: bfloat16 [2048, 4096], P('dp', 'expert'), may hold values from -6 to 6
- gate_prob: float32 [2048, 8], P('dp'), may hold values from 0.05 to 1
- routes: int32 [2048, 8], P('dp'), may hold values from 0 to 63, all different within a row; in each aligned block of 32 rows (0 to 31, 32 to 63, ...) at most 8 rows name the same one
- slot_expert: int32 [64], replicated, may hold values from 0 to 62, as said below
- saved_input: bfloat16 [64, 512, 4096], P('dp', None, 'expert'), may hold values from -6 to 6
- gate_weight: bfloat16 [64, 4096, 1024], P('dp', 'expert'), as said below
- up_weight: bfloat16 [64, 4096, 1024], P('dp', 'expert'), as said below
- down_weight: bfloat16 [64, 1024, 4096], P('dp', None, 'expert'), as said below
Outputs:
- grad_input: bfloat16 [2048, 4096], P('dp', 'expert')
- grad_gate_w: bfloat16 [64, 4096, 1024], P('dp', 'expert')
- grad_up_w: bfloat16 [64, 4096, 1024], P('dp', 'expert')
- grad_down_w: bfloat16 [64, 1024, 4096], P('dp', None, 'expert')
Inputs may be any that keep to these rules, and one draw needn't show every extreme that they name: `routes`: each row names 8 different slots; in the rows of one dp index (32 aligned rows) no slot is named by more than 8 rows, a bound that some block reaches. `slot_expert`: slots s and s + 32 form a pair; the two slots of a pair serve one expert or two experts that no other slot serves; slots 0 and 32 serve one expert, the other pairs vary. `gate_weight`: the two slots of a pair that serve one expert hold equal weights. `up_weight`: the two slots of a pair that serve one expert hold equal weights. `down_weight`: the two slots of a pair that serve one expert hold equal weights.
All inputs are finite; a program needn't handle non-finite values.
Results may differ from a plain program's by a relative error of at most 0.03.
Values may be sent and summed in bfloat16 or wider, within the bound.
A program may use at most 32 MiB of HBM per device.

v0:
```python
import jax
import jax.numpy as jnp
from jax import lax
from jax.sharding import PartitionSpec as P


def partner_2(value, axis, bit):
    mask = 2**bit
    pairs = [(source, source ^ mask) for source in range(lax.axis_size(axis))]
    return lax.ppermute(value, axis, pairs)


def contract(left, right, left_dim, right_dim):
    return lax.dot_general(
        left, right, (((left_dim,), (right_dim,)), ((), ())), preferred_element_type=jnp.float32
    )


def local(
    grad_out, gate_prob, routes, slot_expert, saved_input, gate_weight, up_weight, down_weight
):
    tok_rows, width_part = grad_out.shape
    fanout = routes.shape[1]
    slot_count = lax.axis_size("dp")
    capacity = saved_input.shape[1] // slot_count
    flat_routes = routes.reshape(-1)
    chosen = (flat_routes[:, None] == jnp.arange(slot_count, dtype=jnp.int32)[None, :]).astype(
        jnp.int32
    )
    earlier = jnp.cumsum(chosen, axis=0) - chosen
    position = jnp.sum(earlier * chosen, axis=1)
    target = flat_routes * capacity + position
    select = (
        jnp.arange(slot_count * capacity, dtype=jnp.int32)[:, None] == target[None, :]
    ).astype(jnp.bfloat16)
    inputs = saved_input[0]
    gate_w = gate_weight[0]
    up_w = up_weight[0]
    down_w = down_weight[0]
    gate_part = contract(inputs, gate_w, 1, 0)
    up_part = contract(inputs, up_w, 1, 0)
    scaled = (gate_prob[:, :, None] * grad_out[:, None, :].astype(jnp.float32)).astype(jnp.bfloat16)
    scaled = scaled.reshape(tok_rows * fanout, width_part)
    placed = jnp.dot(select, scaled, preferred_element_type=jnp.float32).astype(jnp.bfloat16)
    arrived = lax.all_to_all(
        placed.reshape(slot_count, capacity, width_part),
        "dp",
        split_axis=0,
        concat_axis=0,
        tiled=True,
    )
    grad_rows = arrived.reshape(slot_count * capacity, width_part)
    act_part = contract(grad_rows, down_w, 1, 1)
    gate_pre, up_pre, grad_act = (
        lax.psum_scatter(
            gate_part.astype(jnp.bfloat16), "expert", scatter_dimension=0, tiled=True
        ).astype(jnp.float32),
        lax.psum_scatter(
            up_part.astype(jnp.bfloat16), "expert", scatter_dimension=0, tiled=True
        ).astype(jnp.float32),
        lax.psum_scatter(
            act_part.astype(jnp.bfloat16), "expert", scatter_dimension=0, tiled=True
        ).astype(jnp.float32),
    )
    sigmoid_gate = jax.nn.sigmoid(gate_pre)
    gated = gate_pre * sigmoid_gate
    activated = (gated * up_pre).astype(jnp.bfloat16)
    grad_up = (grad_act * gated).astype(jnp.bfloat16)
    grad_gate = (grad_act * up_pre * sigmoid_gate * (1.0 + gate_pre * (1.0 - sigmoid_gate))).astype(
        jnp.bfloat16
    )
    full_gate, full_up, full_act = (
        lax.all_gather(grad_gate, "expert", axis=0, tiled=True),
        lax.all_gather(grad_up, "expert", axis=0, tiled=True),
        lax.all_gather(activated, "expert", axis=0, tiled=True),
    )
    returned = (contract(full_gate, gate_w, 1, 1) + contract(full_up, up_w, 1, 1)).astype(
        jnp.bfloat16
    )
    back = lax.all_to_all(
        returned.reshape(slot_count, capacity, width_part),
        "dp",
        split_axis=0,
        concat_axis=0,
        tiled=True,
    )
    picked = contract(select, back.reshape(slot_count * capacity, width_part), 0, 0)
    grad_input = jnp.sum(picked.reshape(tok_rows, fanout, width_part), axis=1).astype(jnp.bfloat16)
    part_gate = contract(inputs, full_gate, 0, 0)
    part_up = contract(inputs, full_up, 0, 0)
    part_down = contract(full_act, grad_rows, 0, 0)
    my_slot = lax.axis_index("dp")
    half_count = slot_count // 2
    partner = jnp.where(my_slot < half_count, my_slot + half_count, my_slot - half_count)
    shared = (slot_expert[my_slot] == slot_expert[partner]).astype(jnp.float32)
    top_bit = slot_count.bit_length() - 2
    received = partner_2(
        (
            part_gate.astype(jnp.bfloat16),
            part_up.astype(jnp.bfloat16),
            part_down.astype(jnp.bfloat16),
        ),
        "dp",
        top_bit,
    )
    grad_gate_w = (part_gate + shared * received[0].astype(jnp.float32)).astype(jnp.bfloat16)
    grad_up_w = (part_up + shared * received[1].astype(jnp.float32)).astype(jnp.bfloat16)
    grad_down_w = (part_down + shared * received[2].astype(jnp.float32)).astype(jnp.bfloat16)
    return (grad_input, grad_gate_w[None], grad_up_w[None], grad_down_w[None])


def solution(mesh):
    placed = (
        P("dp", "expert"),
        P("dp", None),
        P("dp", None),
        P(),
        P("dp", None, "expert"),
        P("dp", "expert", None),
        P("dp", "expert", None),
        P("dp", None, "expert"),
    )
    return jax.shard_map(
        local,
        mesh=mesh,
        in_specs=placed,
        out_specs=(
            P("dp", "expert"),
            P("dp", "expert", None),
            P("dp", "expert", None),
            P("dp", None, "expert"),
        ),
        check_vma=False,
    )
```

profile of v0, /device:TPU:1, one launch (start us, length us, event | category | flops | bytes accessed | tf_op | source)
XLA Modules:
  0.0 1035.9 jit_solution(6451802961458730403)
XLA Ops:
  7.2 0.0 copy-start
  7.2 0.0 copy-start.3
  7.2 0.0 reduce-scatter.6.cloned.1.call-start
  7.2 2.6 convolution_convert_fusion.1
  9.8 0.0 reduce-scatter.6.cloned.1.call-update
  9.9 0.0 copy-start.7
  9.9 0.0 reduce-scatter.8.cloned.1.call-start
  9.9 0.0 copy-done
  9.9 0.0 copy-done.3
  9.9 1.4 convolution_convert_fusion
  11.4 0.0 reduce-scatter.8.cloned.1.call-update
  11.4 0.0 reduce-scatter.4.cloned.1.call-start
  11.5 0.0 copy-done.7
  11.5 0.1 copy.14
  11.6 0.1 reshape.84
  11.6 0.1 eq.59
  11.8 0.6 reduce-window.6
  12.4 0.2 slice_reduce_fusion
  12.6 0.0 copy-done.8
  12.6 0.1 copy.17
  12.7 0.1 mul.71
  12.8 0.1 fusion.39
  12.9 0.3 fusion.1
  13.2 29.1 %all_to_all.10 = bf16[64,8,256]{2,1,0:T(8,128)(2,1)S(1)} all-to-all(bf16[64,8,256]{2,1,0:T(8,128)(2,1)S(1)} %fusion.1), channel_id=1, replica_groups=mesh['expert'=16,'dp'=64] {'dp'}, dimensions={0} | all-to-all | bytes 524288 | tf_op jit(solution)/shard_map/all_to_all | solution.py:45
  42.4 1.4 convolution_convert_fusion.2
  43.8 0.0 reduce-scatter.4.cloned.1.call-update
  43.8 0.0 all-gather.4.cloned.1.call-start
  43.9 204.6 %reduce-scatter.6.cloned.1.call-done = bf16[32,1024]{1,0:T(8,128)(2,1)} async-done(((bf16[512,1024]{1,0:T(8,128)(2,1)}), bf16[32,1024]{1,0:T(8,128)(2,1)}) %reduce-scatter.6.cloned.1.call-update) | async-done | bytes 65552 | tf_op jit(solution)/shard_map/reduce_scatter | solution.py:58
  248.4 227.9 %reduce-scatter.8.cloned.1.call-done = bf16[32,1024]{1,0:T(8,128)(2,1)} async-done(((bf16[512,1024]{1,0:T(8,128)(2,1)}), bf16[32,1024]{1,0:T(8,128)(2,1)}) %reduce-scatter.8.cloned.1.call-update) | async-done | bytes 65552 | tf_op jit(solution)/shard_map/reduce_scatter | solution.py:55
  476.3 227.9 %reduce-scatter.4.cloned.1.call-done = bf16[32,1024]{1,0:T(8,128)(2,1)} async-done(((bf16[512,1024]{1,0:T(8,128)(2,1)}), bf16[32,1024]{1,0:T(8,128)(2,1)}) %reduce-scatter.4.cloned.1.call-update) | async-done | bytes 65552 | tf_op jit(solution)/shard_map/reduce_scatter | solution.py:61
  704.2 1.7 fusion.29
  705.8 0.0 all-gather.4.cloned.1.call-update
  705.8 0.0 all-gather.6.cloned.1.call-start
  705.9 0.5 all-gather.6.cloned.1.call-update
  706.4 0.0 all-gather.8.cloned.1.call-start
  706.5 0.5 all-gather.8.cloned.1.call-update
  707.0 0.0 copy-done.9
  707.0 0.6 fusion.41
  708.9 0.0 copy-start.4
  708.9 92.4 %all-gather.4.cloned.1.call-done = bf16[512,1024]{1,0:T(8,128)(2,1)} async-done(((bf16[32,1024]{1,0:T(8,128)(2,1)}), bf16[512,1024]{1,0:T(8,128)(2,1)}) %all-gather.4.cloned.1.call-update) | async-done | bytes 1048592 | tf_op jit(solution)/shard_map/all_gather | solution.py:73
  801.3 1.7 fusion.6
  803.0 0.0 copy-start.1
  803.0 95.8 %all-gather.6.cloned.1.call-done = bf16[512,1024]{1,0:T(8,128)(2,1)} async-done(((bf16[32,1024]{1,0:T(8,128)(2,1)}), bf16[512,1024]{1,0:T(8,128)(2,1)}) %all-gather.6.cloned.1.call-update) | async-done | bytes 1048592 | tf_op jit(solution)/shard_map/all_gather | solution.py:74
  898.8 2.4 fusion.2
  901.2 15.2 %all-to-all-start.1 = ((bf16[64,8,256]{2,1,0:T(8,128)(2,1)}), bf16[64,8,256]{2,1,0:T(8,128)(2,1)S(1)}, u32[]{:S(2)}, u32[]{:S(2)}) async-start(bf16[64,8,256]{2,1,0:T(8,128)(2,1)} %fusion.2), calls=%async_computation.4 | async-start | bytes 524288 | tf_op jit(solution)/shard_map/all_to_all | solution.py:80
  916.5 0.0 copy-done.1
  916.5 0.0 copy-start.2
  916.5 1.6 fusion.42
  918.1 4.3 collective-permute-start
  922.4 1.3 fusion.43
  923.7 1.9 collective-permute-start.1
  925.6 69.2 %all-gather.8.cloned.1.call-done = bf16[512,1024]{1,0:T(8,128)(2,1)} async-done(((bf16[32,1024]{1,0:T(8,128)(2,1)}), bf16[512,1024]{1,0:T(8,128)(2,1)}) %all-gather.8.cloned.1.call-update) | async-done | bytes 1048592 | tf_op jit(solution)/shard_map/all_gather | solution.py:75
  994.8 2.5 fusion.44
  997.3 7.7 collective-permute-start.2
  1005.0 0.0 all-to-all-done.1
  1005.0 0.9 convolution_reduce_fusion
  1005.9 0.0 collective-permute-done
  1005.9 1.5 fusion.3
  1007.4 1.0 copy.18
  1008.4 0.0 collective-permute-done.1
  1008.4 1.2 fusion.4
  1009.6 1.0 copy.19
  1010.6 16.5 %collective-permute-done.2 = bf16[1024,256]{1,0:T(8,128)(2,1)} collective-permute-done((bf16[1024,256]{1,0:T(8,128)(2,1)}, bf16[1024,256]{1,0:T(8,128)(2,1)}, u32[]{:S(2)}, u32[]{:S(2)}) %collective-permute-start.2) | collective-permute-done | bytes 524320 | tf_op jit(solution)/shard_map/ppermute | solution.py:10
  1027.1 2.0 fusion.5
  (13 shorter events, 0.1 us)
Async XLA Ops:
  7.2 2.8 copy-start
  7.2 2.8 copy-start.3
  7.2 241.3 %reduce-scatter.6.cloned.1.call-start = ((), (), s32[]{:S(2)}) async-start(), calls=%async_computation.6 | async-start | bytes 1114112 | tf_op jit(solution)/shard_map/reduce_scatter | solution.py:58
  9.9 1.6 copy-start.7
  9.9 466.4 %reduce-scatter.8.cloned.1.call-start = ((), (), s32[]{:S(2)}) async-start(), calls=%async_computation.7 | async-start | bytes 1114112 | tf_op jit(solution)/shard_map/reduce_scatter | solution.py:55
  11.4 1.2 copy-start.6
  11.4 1.2 copy-start.8
  11.4 31.0 %copy-start.5 = (bf16[1,1024,256]{2,1,0:T(8,128)(2,1)S(1)}, bf16[1,1024,256]{2,1,0:T(8,128)(2,1)}, u32[]{:S(2)}) copy-start(bf16[1,1024,256]{2,1,0:T(8,128)(2,1)} %param.15) | copy-start | bytes 1572868
  11.4 692.7 %reduce-scatter.4.cloned.1.call-start = ((), (), s32[]{:S(2)}) async-start(), calls=%async_computation.5 | async-start | bytes 1114112 | tf_op jit(solution)/shard_map/reduce_scatter | solution.py:61
  43.8 663.2 %copy-start.9 = (s32[64]{0:T(128)S(1)}, s32[64]{0:T(128)}, u32[]{:S(2)}) copy-start(s32[64]{0:T(128)} %param.11) | copy-start | bytes 772
  43.8 757.5 %all-gather.4.cloned.1.call-start = ((), (), s32[]{:S(2)}) async-start(), calls=%async_computation.8 | async-start | bytes 1114112 | tf_op jit(solution)/shard_map/all_gather | solution.py:73
  705.8 193.0 %all-gather.6.cloned.1.call-start = ((), (), s32[]{:S(2)}) async-start(), calls=%async_computation.9 | async-start | bytes 1114112 | tf_op jit(solution)/shard_map/all_gather | solution.py:74
  706.4 288.4 %all-gather.8.cloned.1.call-start = ((), (), s32[]{:S(2)}) async-start(), calls=%async_computation.10 | async-start | bytes 1114112 | tf_op jit(solution)/shard_map/all_gather | solution.py:75
  708.9 189.9 %copy-start.4 = (bf16[1,256,1024]{2,1,0:T(8,128)(2,1)S(1)}, bf16[1,256,1024]{2,1,0:T(8,128)(2,1)}, u32[]{:S(2)}) copy-start(bf16[1,256,1024]{2,1,0:T(8,128)(2,1)} %param.14) | copy-start | bytes 1572868
  803.0 113.5 %copy-start.1 = (bf16[512,1024]{1,0:T(8,128)(2,1)S(1)}, bf16[512,1024]{1,0:T(8,128)(2,1)}, u32[]{:S(2)}) copy-start(bf16[512,1024]{1,0:T(8,128)(2,1)} %all-gather.4.cloned.1.call-done) | copy-start | bytes 3145732
  901.2 103.8 %all-to-all-start.1 = ((bf16[64,8,256]{2,1,0:T(8,128)(2,1)}), bf16[64,8,256]{2,1,0:T(8,128)(2,1)S(1)}, u32[]{:S(2)}, u32[]{:S(2)}) async-start(bf16[64,8,256]{2,1,0:T(8,128)(2,1)} %fusion.2), calls=%async_computation.4 | async-start | bytes 524288 | tf_op jit(solution)/shard_map/all_to_all | solution.py:80
  916.5 5.9 copy-start.2
  918.1 87.8 %collective-permute-start = (bf16[256,1024]{0,1:T(8,128)(2,1)}, bf16[256,1024]{0,1:T(8,128)(2,1)}, u32[]{:S(2)}, u32[]{:S(2)}) collective-permute-start(bf16[256,1024]{0,1:T(8,128)(2,1)} %get-tuple-element.17), channel_id=1, source_target_pairs={{0,32},{1,33},{2,34},{3,35},{4,36},{5,37},{6,38},{7,39},{8,40},{9,... | collective-permute-start | bytes 1572872 | tf_op jit(solution)/shard_map/ppermute | solution.py:10
  923.7 84.7 %collective-permute-start.1 = (bf16[256,1024]{0,1:T(8,128)(2,1)}, bf16[256,1024]{0,1:T(8,128)(2,1)}, u32[]{:S(2)}, u32[]{:S(2)}) collective-permute-start(bf16[256,1024]{0,1:T(8,128)(2,1)} %get-tuple-element.19), channel_id=1, source_target_pairs={{0,32},{1,33},{2,34},{3,35},{4,36},{5,37},{6,38},{7,39},{8,40},{9,... | collective-permute-start | bytes 1572872 | tf_op jit(solution)/shard_map/ppermute | solution.py:10
  997.3 29.8 %collective-permute-start.2 = (bf16[1024,256]{1,0:T(8,128)(2,1)}, bf16[1024,256]{1,0:T(8,128)(2,1)}, u32[]{:S(2)}, u32[]{:S(2)}) collective-permute-start(bf16[1024,256]{1,0:T(8,128)(2,1)} %get-tuple-element.21), channel_id=1, source_target_pairs={{0,32},{1,33},{2,34},{3,35},{4,36},{5,37},{6,38},{7,39},{8,40},{9,... | collective-permute-start | bytes 1572872 | tf_op jit(solution)/shard_map/ppermute | solution.py:10
Sparse Core Ops, SparseCore 0:
  13.6 234.7 reduce-scatter.5
  254.0 222.2 reduce-scatter.7
  481.9 222.2 reduce-scatter.3
  708.9 92.3 all-gather.3
  806.1 92.7 all-gather.5
  903.0 91.7 all-gather.7
where the time goes:
time: 1040 us
  waiting for transfers between devices  935 us (90%)
  starting transfers between devices  29.3 us (3%)
  blocking collectives  29.1 us (3%)
  matrix products  16.2 us (2%)
  between operations  15.6 us (2%)
    reduce_scatter x1, waiting for transfers between devices, local(): lax.psum_scatter(gate_part.astype(jnp.bfloat16), 'expert', scatter_dimens...  228 us
    reduce_scatter x1, waiting for transfers between devices, local(): lax.psum_scatter(act_part.astype(jnp.bfloat16), 'expert', scatter_dimensi...  228 us
    reduce_scatter x1, waiting for transfers between devices, local(): lax.psum_scatter(up_part.astype(jnp.bfloat16), 'expert', scatter_dimensio...  205 us
    all_gather x1, waiting for transfers between devices, local(): lax.all_gather(grad_up, 'expert', axis=0, tiled=True)  95.8 us
    all_gather x1, waiting for transfers between devices, local(): lax.all_gather(grad_gate, 'expert', axis=0, tiled=True)  92.4 us
    all_gather x1, waiting for transfers between devices, local(): lax.all_gather(activated, 'expert', axis=0, tiled=True)  69.2 us
    all_to_all x1, blocking collectives, local(): lax.all_to_all(placed.reshape(slot_count, capacity, width_part), 'dp', sp...  29.1 us
  transfers between devices with their start and end apart: 10, of which 7 were waited for; matrix products, arithmetic and copies ran while one was open for 2% of the time, Pallas kernels for 0%

commit v1 on v0

v1 whole, which is shorter than its diff:
```python
import jax
import jax.numpy as jnp
from jax import lax
from jax.experimental import pallas as pl
from jax.experimental.pallas import tpu as pltpu
from jax.sharding import PartitionSpec as P

MESH = pl.DeviceIdType.MESH
GATE, UP, ACT = 0, 1, 2


def contract(left, right, left_dim, right_dim):
    return lax.dot_general(
        left, right, (((left_dim,), (right_dim,)), ((), ())), preferred_element_type=jnp.float32
    )


def slot_kernel(
    shared_ref,
    x_ref,
    rows_ref,
    gate_ref,
    up_ref,
    down_ref,
    returned_ref,
    grad_gate_ref,
    grad_up_ref,
    grad_down_ref,
    ring,
    own,
    swap_out,
    swap_in,
    full,
    other,
    x_other,
    down_out,
    down_in,
    ring_send,
    ring_recv,
    swap_send,
    swap_recv,
    full_send,
    full_recv,
    other_send,
    other_recv,
    pair_send,
    pair_recv,
    x_send,
    x_recv,
    down_send,
    down_recv,
):
    e = lax.axis_index("expert")
    d = lax.axis_index("dp")
    nz = lax.axis_size("expert") // 2
    ndp = lax.axis_size("dp")
    z, h = e // 2, e % 2
    rows = x_ref.shape[0] // nz
    half = gate_ref.shape[1] // 2
    step_of = (1, nz - 1)
    to = tuple((((z + k) % nz) * 2 + h, d) for k in step_of)
    twin = (z * 2 + (1 - h), d)
    pair = (e, (d + ndp // 2) % ndp)

    barrier = pltpu.get_barrier_semaphore()
    for device in (to[0], to[1], twin, pair):
        pl.semaphore_signal(barrier, inc=1, device_id=device, device_id_type=MESH)
    pl.semaphore_wait(barrier, 4)

    def remote(src, dst, send, recv, device):
        return pltpu.make_async_remote_copy(
            src_ref=src, dst_ref=dst, send_sem=send, recv_sem=recv, device_id=device, device_id_type=MESH
        )

    def block(index):
        return pl.ds(pl.multiple_of(index * rows, rows), rows)

    def term(a, way, index):
        cols = pl.ds(way * half, half)
        if a == GATE:
            return contract(x_ref[block(index), :], gate_ref[:, cols], 1, 0)
        if a == UP:
            return contract(x_ref[block(index), :], up_ref[:, cols], 1, 0)
        return contract(rows_ref[block(index), :], down_ref[cols, :], 1, 1)

    def ring_copy(a, way, s):
        return remote(
            ring.at[a, way, s], ring.at[a, way, s + 1], ring_send.at[a, way, s], ring_recv.at[a, way, s], to[way]
        )

    def chunk(way, s):
        return (z + (nz - 1 - s if way == 0 else 1 + s)) % nz

    everything = [(a, way) for a in (GATE, UP, ACT) for way in (0, 1)]
    for a, way in everything:
        ring[a, way, 0] = term(a, way, chunk(way, 0)).astype(jnp.bfloat16)
        ring_copy(a, way, 0).start()
    x_copy = remote(x_ref, x_other, x_send, x_recv, pair)
    x_copy.start()

    def ring_step(s, carry):
        for a, way in everything:
            mine = term(a, way, chunk(way, s + 1))
            ring_copy(a, way, s).wait_recv()
            ring[a, way, s + 1] = (ring[a, way, s + 1].astype(jnp.float32) + mine).astype(jnp.bfloat16)
            ring_copy(a, way, s + 1).start()
        return carry

    lax.fori_loop(0, nz - 2, ring_step, 0)

    def swap_copy(a, way):
        return remote(swap_out.at[a, way], swap_in.at[a, way], swap_send.at[a, way], swap_recv.at[a, way], twin)

    for a, way in everything:
        mine = term(a, way, z)
        ring_copy(a, way, nz - 2).wait_recv()
        total = ring[a, way, nz - 1].astype(jnp.float32) + mine
        own[a, way] = total
        swap_out[a, way] = total.astype(jnp.bfloat16)
        swap_copy(a, way).start()

    def full_copy(a, way, s):
        at = block((z + (nz - s if way == 0 else s)) % nz)
        return remote(
            full.at[a, way, at, :], full.at[a, way, at, :], full_send.at[a, way, s], full_recv.at[a, way, s], to[way]
        )

    def other_copy(a, way, s):
        at = block((z + (nz - s if way == 0 else s)) % nz)
        return remote(
            other.at[a, way, at, :],
            other.at[a, way, at, :],
            other_send.at[a, way, s],
            other_recv.at[a, way, s],
            to[way],
        )

    def pair_copy(a, way):
        at = block(z)
        return remote(
            full.at[a, way, at, :], other.at[a, way, at, :], pair_send.at[a, way], pair_recv.at[a, way], pair
        )

    for way in (0, 1):
        value = []
        for a in (GATE, UP, ACT):
            swap_copy(a, way).wait_recv()
            value.append(own[a, way] + swap_in[a, way].astype(jnp.float32))
        gate_pre, up_pre, grad_act = value
        sigmoid_gate = jax.nn.sigmoid(gate_pre)
        gated = gate_pre * sigmoid_gate
        full[ACT, way, block(z), :] = (gated * up_pre).astype(jnp.bfloat16)
        full_copy(ACT, way, 0).start()
        full[GATE, way, block(z), :] = (
            grad_act * up_pre * sigmoid_gate * (1.0 + gate_pre * (1.0 - sigmoid_gate))
        ).astype(jnp.bfloat16)
        full_copy(GATE, way, 0).start()
        full[UP, way, block(z), :] = (grad_act * gated).astype(jnp.bfloat16)
        full_copy(UP, way, 0).start()
        pair_copy(GATE, way).start()
        pair_copy(UP, way).start()

    def full_step(s, carry):
        for a in (ACT, GATE, UP):
            for way in (0, 1):
                full_copy(a, way, s).wait_recv()
                full_copy(a, way, s + 1).start()
        return carry

    lax.fori_loop(0, nz - 2, full_step, 0)

    for a in (GATE, UP):
        for way in (0, 1):
            pair_copy(a, way).wait_recv()
            other_copy(a, way, 0).start()

    down_copy = [
        remote(down_out.at[way], down_in.at[way], down_send.at[way], down_recv.at[way], pair) for way in (0, 1)
    ]
    for way in (0, 1):
        full_copy(ACT, way, nz - 2).wait_recv()
        part = contract(full[ACT, way], rows_ref[...], 0, 0)
        grad_down_ref[pl.ds(way * half, half), :] = part.astype(jnp.bfloat16)
        down_out[way] = part.astype(jnp.bfloat16)
        down_copy[way].start()
    for a in (GATE, UP):
        for way in (0, 1):
            full_copy(a, way, nz - 2).wait_recv()
    returned_ref[...] = sum(
        contract(full[a, way], w[:, pl.ds(way * half, half)], 1, 1)
        for a, w in ((GATE, gate_ref), (UP, up_ref))
        for way in (0, 1)
    ).astype(jnp.bfloat16)

    def other_step(s, carry):
        for a in (GATE, UP):
            for way in (0, 1):
                other_copy(a, way, s).wait_recv()
                other_copy(a, way, s + 1).start()
        return carry

    lax.fori_loop(0, nz - 2, other_step, 0)

    x_copy.wait_recv()
    shared = shared_ref[0:1, 0:1]
    for a, out in ((GATE, grad_gate_ref), (UP, grad_up_ref)):
        for way in (0, 1):
            part = contract(x_ref[...], full[a, way], 0, 0)
            other_copy(a, way, nz - 2).wait_recv()
            part = part + shared * contract(x_other[...], other[a, way], 0, 0)
            out[:, pl.ds(way * half, half)] = part.astype(jnp.bfloat16)
    for way in (0, 1):
        at = pl.ds(way * half, half)
        down_copy[way].wait_recv()
        grad_down_ref[at, :] = (
            grad_down_ref[at, :].astype(jnp.float32) + shared * down_in[way].astype(jnp.float32)
        ).astype(jnp.bfloat16)

    x_copy.wait_send()
    for way in (0, 1):
        down_copy[way].wait_send()
        for a in (GATE, UP, ACT):
            swap_copy(a, way).wait_send()
        for a in (GATE, UP):
            pair_copy(a, way).wait_send()

    def drain(s, carry):
        for a, way in everything:
            ring_copy(a, way, s).wait_send()
            full_copy(a, way, s).wait_send()
            if a != ACT:
                other_copy(a, way, s).wait_send()
        return carry

    lax.fori_loop(0, nz - 1, drain, 0)


def slot_call(shared, x, rows, gate_w, up_w, down_w):
    nz = lax.axis_size("expert") // 2
    count, width = x.shape
    hidden = gate_w.shape[1]
    half = hidden // 2
    part = count // nz
    bf16, f32 = jnp.bfloat16, jnp.float32
    vmem = pl.BlockSpec(memory_space=pltpu.VMEM)
    dma = pltpu.SemaphoreType.DMA
    return pl.pallas_call(
        slot_kernel,
        out_shape=(
            jax.ShapeDtypeStruct((count, width), bf16),
            jax.ShapeDtypeStruct((width, hidden), bf16),
            jax.ShapeDtypeStruct((width, hidden), bf16),
            jax.ShapeDtypeStruct((hidden, width), bf16),
        ),
        in_specs=[vmem] * 6,
        out_specs=(vmem,) * 4,
        scratch_shapes=[
            pltpu.VMEM((3, 2, nz, part, half), bf16),
            pltpu.VMEM((3, 2, part, half), f32),
            pltpu.VMEM((3, 2, part, half), bf16),
            pltpu.VMEM((3, 2, part, half), bf16),
            pltpu.VMEM((3, 2, count, half), bf16),
            pltpu.VMEM((2, 2, count, half), bf16),
            pltpu.VMEM((count, width), bf16),
            pltpu.VMEM((2, half, width), bf16),
            pltpu.VMEM((2, half, width), bf16),
            dma((3, 2, nz - 1)),
            dma((3, 2, nz - 1)),
            dma((3, 2)),
            dma((3, 2)),
            dma((3, 2, nz - 1)),
            dma((3, 2, nz - 1)),
            dma((2, 2, nz - 1)),
            dma((2, 2, nz - 1)),
            dma((2, 2)),
            dma((2, 2)),
            dma,
            dma,
            dma((2,)),
            dma((2,)),
        ],
        compiler_params=pltpu.CompilerParams(
            collective_id=0, has_side_effects=True, vmem_limit_bytes=40 * 1024 * 1024
        ),
    )(shared, x, rows, gate_w, up_w, down_w)


def local(
    grad_out, gate_prob, routes, slot_expert, saved_input, gate_weight, up_weight, down_weight
):
    tok_rows, width_part = grad_out.shape
    fanout = routes.shape[1]
    slot_count = lax.axis_size("dp")
    capacity = saved_input.shape[1] // slot_count
    flat_routes = routes.reshape(-1)
    chosen = (flat_routes[:, None] == jnp.arange(slot_count, dtype=jnp.int32)[None, :]).astype(
        jnp.int32
    )
    earlier = jnp.cumsum(chosen, axis=0) - chosen
    position = jnp.sum(earlier * chosen, axis=1)
    target = flat_routes * capacity + position
    select = (
        jnp.arange(slot_count * capacity, dtype=jnp.int32)[:, None] == target[None, :]
    ).astype(jnp.bfloat16)
    scaled = (gate_prob[:, :, None] * grad_out[:, None, :].astype(jnp.float32)).astype(jnp.bfloat16)
    scaled = scaled.reshape(tok_rows * fanout, width_part)
    placed = jnp.dot(select, scaled, preferred_element_type=jnp.float32).astype(jnp.bfloat16)
    arrived = lax.all_to_all(
        placed.reshape(slot_count, capacity, width_part),
        "dp",
        split_axis=0,
        concat_axis=0,
        tiled=True,
    )
    grad_rows = arrived.reshape(slot_count * capacity, width_part)
    my_slot = lax.axis_index("dp")
    partner = (my_slot + slot_count // 2) % slot_count
    shared = (slot_expert[my_slot] == slot_expert[partner]).astype(jnp.float32)
    returned, grad_gate_w, grad_up_w, grad_down_w = slot_call(
        jnp.full((8, 128), shared, jnp.float32),
        saved_input[0],
        grad_rows,
        gate_weight[0],
        up_weight[0],
        down_weight[0],
    )
    back = lax.all_to_all(
        returned.reshape(slot_count, capacity, width_part),
        "dp",
        split_axis=0,
        concat_axis=0,
        tiled=True,
    )
    picked = contract(select, back.reshape(slot_count * capacity, width_part), 0, 0)
    grad_input = jnp.sum(picked.reshape(tok_rows, fanout, width_part), axis=1).astype(jnp.bfloat16)
    return (grad_input, grad_gate_w[None], grad_up_w[None], grad_down_w[None])


def solution(mesh):
    placed = (
        P("dp", "expert"),
        P("dp", None),
        P("dp", None),
        P(),
        P("dp", None, "expert"),
        P("dp", "expert", None),
        P("dp", "expert", None),
        P("dp", None, "expert"),
    )
    return jax.shard_map(
        local,
        mesh=mesh,
        in_specs=placed,
        out_specs=(
            P("dp", "expert"),
            P("dp", "expert", None),
            P("dp", "expert", None),
            P("dp", None, "expert"),
        ),
        check_vma=False,
    )
```

time: 1040 us -> 179 us (0.17)
  waiting for transfers between devices: 935 us -> 21.5 us
  Pallas kernels: 0 us -> 114 us
  blocking collectives: 29.1 us -> 0 us
  matrix products: 16.2 us -> 1.93 us
  between operations: 15.6 us -> 2.05 us
    reduce_scatter x3 -> x0, waiting for transfers between devices: 660 us -> none  [the longest x1 228 us: local(): lax.psum_scatter(gate_part.astype(jnp.bfloat16), 'expert', scatter_dimens...]
    all_gather x3 -> x0, waiting for transfers between devices: 257 us -> none  [the longest x1 95.8 us: local(): lax.all_gather(grad_up, 'expert', axis=0, tiled=True)]
    pallas_call x0 -> x1, Pallas kernels: none -> 114 us  [slot_call(): pl.pallas_call(slot_kernel, out_shape=(jax.ShapeDtypeStruct((count, width...]
    all_to_all x1 -> x0, blocking collectives: 29.1 us -> none  [local(): lax.all_to_all(placed.reshape(slot_count, capacity, width_part), 'dp', sp...]
    all_to_all x0 -> x1, starting transfers between devices: none -> 18.2 us  [local(): lax.all_to_all(placed.reshape(slot_count, capacity, width_part), 'dp', sp...]
    ppermute x3 -> x0, waiting for transfers between devices: 16.6 us -> none  [partner_2(): return lax.ppermute(value, axis, pairs)]
    dot_general x9 -> x1, matrix products: 15.9 us -> 0.9 us  [contract(): lax.dot_general(left, right, (((left_dim,), (right_dim,)), ((), ())), pre...]
    ppermute x3 -> x0, starting transfers between devices: 13.9 us -> none  [partner_2(): return lax.ppermute(value, axis, pairs)]
  transfers between devices with their start and end apart: 10 -> 2, of which waited for: 7 -> 2; matrix products, arithmetic and copies ran while one was open for 2% -> 0% of each run, Pallas kernels for 0% -> 0%
where the time goes in v1:
time: 179 us
  Pallas kernels  114 us (64%)
  starting transfers between devices  32.6 us (18%)
  waiting for transfers between devices  21.5 us (12%)
  local copies, waits for them, and re-layouts  5.86 us (3%)
  between operations  2.05 us (1%)
  matrix products  1.93 us (1%)
    pallas_call x1, Pallas kernels, slot_call(): pl.pallas_call(slot_kernel, out_shape=(jax.ShapeDtypeStruct((count, width...  114 us
    all_to_all x1, starting transfers between devices, local(): lax.all_to_all(placed.reshape(slot_count, capacity, width_part), 'dp', sp...  18.2 us
    all_to_all x1, starting transfers between devices, local(): lax.all_to_all(returned.reshape(slot_count, capacity, width_part), 'dp',...  14.4 us
    all_to_all x1, waiting for transfers between devices, local(): lax.all_to_all(returned.reshape(slot_count, capacity, width_part), 'dp',...  11.6 us
    all_to_all x1, waiting for transfers between devices, local(): lax.all_to_all(placed.reshape(slot_count, capacity, width_part), 'dp', sp...  9.83 us
    unnamed x19, local copies, waits for them, and re-layouts  4.82 us
  transfers between devices with their start and end apart: 2, of which 2 were waited for; matrix products, arithmetic and copies ran while one was open for 0% of the time, Pallas kernels for 0%

profile of v1, /device:TPU:1, one launch (start us, length us, event | category | flops | bytes accessed | tf_op | source)
XLA Modules:
  0.0 178.9 jit_solution(5992246036565551962)
XLA Ops:
  0.6 0.8 copy.12
  1.4 0.1 reshape.84
  1.5 0.1 eq.61
  1.6 0.0 copy-start.3
  1.6 0.6 reduce-window.6
  2.2 0.0 copy-start.6
  2.2 0.2 slice_reduce_fusion
  2.4 0.0 copy-start.4
  2.4 0.0 copy-start.5
  2.5 0.0 copy-start
  2.5 0.0 copy-start.1
  2.5 0.1 fusion.12
  2.6 0.5 copy-done.4
  3.1 0.0 copy-done.5
  3.1 0.1 copy.15
  3.2 0.1 mul.34
  3.3 1.0 fusion
  4.3 18.2 %all-to-all-start = ((bf16[64,8,256]{2,1,0:T(8,128)(2,1)}), bf16[64,8,256]{2,1,0:T(8,128)(2,1)S(1)}, u32[]{:S(2)}, u32[]{:S(2)}) async-start(bf16[64,8,256]{2,1,0:T(8,128)(2,1)} %fusion), calls=%async_computation | async-start | bytes 524288 | tf_op jit(solution)/shard_map/all_to_all | solution.py:308
  22.6 0.0 copy-done.6
  22.6 0.6 fusion.14
  24.5 9.8 %all-to-all-done = bf16[64,8,256]{2,1,0:T(8,128)(2,1)S(1)} async-done(((bf16[64,8,256]{2,1,0:T(8,128)(2,1)}), bf16[64,8,256]{2,1,0:T(8,128)(2,1)S(1)}, u32[]{:S(2)}, u32[]{:S(2)}) %all-to-all-start) | async-done | bytes 262176 | tf_op jit(solution)/shard_map/all_to_all | solution.py:308
  34.3 0.0 copy-done.3
  34.3 0.0 copy-done
  34.3 0.0 copy-done.1
  34.3 0.0 copy-start.2
  34.3 1.0 copy-done.2
  35.3 114.2 %shard_map.111 = (bf16[512,256]{1,0:T(8,128)(2,1)}, bf16[256,1024]{1,0:T(8,128)(2,1)S(1)}, bf16[256,1024]{1,0:T(8,128)(2,1)S(1)}, bf16[1024,256]{1,0:T(8,128)(2,1)S(1)}) custom-call(f32[8,128]{1,0:T(8,128)S(1)} %broadcast_in_dim.8.shared_ref, bf16[512,256]{1,0:T(8,128)(2,1)S(1)} %bitcast.51, bf16[512,256]{1,0:T(8,128)(2,1)S(1)} %bitcast.44, ...), custom_call_target="tpu_custom_call" | custom-call | tf_op jit(solution)/shard_map/pallas_call | solution.py:247
  149.6 14.4 %all-to-all-start.1 = ((bf16[64,8,256]{2,1,0:T(8,128)(2,1)}), bf16[64,8,256]{2,1,0:T(8,128)(2,1)S(1)}, u32[]{:S(2)}, u32[]{:S(2)}) async-start(bf16[64,8,256]{2,1,0:T(8,128)(2,1)} %bitcast.10), calls=%async_computation.1 | async-start | bytes 524288 | tf_op jit(solution)/shard_map/all_to_all | solution.py:327
  163.9 11.6 %all-to-all-done.1 = bf16[64,8,256]{2,1,0:T(8,128)(2,1)S(1)} async-done(((bf16[64,8,256]{2,1,0:T(8,128)(2,1)}), bf16[64,8,256]{2,1,0:T(8,128)(2,1)S(1)}, u32[]{:S(2)}, u32[]{:S(2)}) %all-to-all-start.1) | async-done | bytes 262176 | tf_op jit(solution)/shard_map/all_to_all | solution.py:327
  175.6 0.9 convolution_reduce_fusion
  176.5 0.8 copy.21
  177.3 0.8 copy.22
  178.1 0.8 copy.23
  (6 shorter events, 0.1 us)
Async XLA Ops:
  1.6 32.7 %copy-start.3 = (bf16[1,512,256]{2,1,0:T(8,128)(2,1)S(1)}, bf16[1,512,256]{2,1,0:T(8,128)(2,1)}, u32[]{:S(2)}) copy-start(bf16[1,512,256]{2,1,0:T(8,128)(2,1)} %param.12) | copy-start | bytes 786436
  2.2 20.3 %copy-start.6 = (s32[64]{0:T(128)S(1)}, s32[64]{0:T(128)}, u32[]{:S(2)}) copy-start(s32[64]{0:T(128)} %param.11) | copy-start | bytes 772
  2.4 0.7 copy-start.4
  2.4 0.7 copy-start.5
  2.5 31.8 %copy-start = (bf16[1,256,1024]{2,1,0:T(8,128)(2,1)S(1)}, bf16[1,256,1024]{2,1,0:T(8,128)(2,1)}, u32[]{:S(2)}) copy-start(bf16[1,256,1024]{2,1,0:T(8,128)(2,1)} %param.13) | copy-start | bytes 1572868
  2.5 31.8 %copy-start.1 = (bf16[1,256,1024]{2,1,0:T(8,128)(2,1)S(1)}, bf16[1,256,1024]{2,1,0:T(8,128)(2,1)}, u32[]{:S(2)}) copy-start(bf16[1,256,1024]{2,1,0:T(8,128)(2,1)} %param.14) | copy-start | bytes 1572868
  4.3 30.0 %all-to-all-start = ((bf16[64,8,256]{2,1,0:T(8,128)(2,1)}), bf16[64,8,256]{2,1,0:T(8,128)(2,1)S(1)}, u32[]{:S(2)}, u32[]{:S(2)}) async-start(bf16[64,8,256]{2,1,0:T(8,128)(2,1)} %fusion), calls=%async_computation | async-start | bytes 524288 | tf_op jit(solution)/shard_map/all_to_all | solution.py:308
  34.3 1.0 copy-start.2
  149.6 26.0 %all-to-all-start.1 = ((bf16[64,8,256]{2,1,0:T(8,128)(2,1)}), bf16[64,8,256]{2,1,0:T(8,128)(2,1)S(1)}, u32[]{:S(2)}, u32[]{:S(2)}) async-start(bf16[64,8,256]{2,1,0:T(8,128)(2,1)} %bitcast.10), calls=%async_computation.1 | async-start | bytes 524288 | tf_op jit(solution)/shard_map/all_to_all | solution.py:327

commit v2 on v1

--- a/solution.py
+++ b/solution.py
@@ -7,6 +7,8 @@
 
 MESH = pl.DeviceIdType.MESH
 GATE, UP, ACT = 0, 1, 2
+FAR = 4
+FIRST, SECOND = 2, 4
 
 
 def contract(left, right, left_dim, right_dim):
@@ -18,15 +20,23 @@
 def slot_kernel(
     shared_ref,
     x_ref,
-    rows_ref,
+    placed_ref,
+    pick_ref,
     gate_ref,
     up_ref,
     down_ref,
-    returned_ref,
+    grad_input_ref,
     grad_gate_ref,
     grad_up_ref,
     grad_down_ref,
+    mid,
+    arrived,
+    rows_ref,
+    going,
+    mid_back,
+    back,
     ring,
+    ring_act,
     own,
     swap_out,
     swap_in,
@@ -35,8 +45,19 @@
     x_other,
     down_out,
     down_in,
+    near_send,
+    near_recv,
+    far_send,
+    far_recv,
+    back_far_send,
+    back_far_recv,
+    back_near_send,
+    back_near_recv,
+    local_sem,
     ring_send,
     ring_recv,
+    act_send,
+    act_recv,
     swap_send,
     swap_recv,
     full_send,
@@ -54,18 +75,20 @@
     d = lax.axis_index("dp")
     nz = lax.axis_size("expert") // 2
     ndp = lax.axis_size("dp")
+    far, near = mid.shape[1], mid.shape[0]
+    dx, dy = d // near, d % near
     z, h = e // 2, e % 2
     rows = x_ref.shape[0] // nz
     half = gate_ref.shape[1] // 2
-    step_of = (1, nz - 1)
-    to = tuple((((z + k) % nz) * 2 + h, d) for k in step_of)
+    to = tuple((((z + k) % nz) * 2 + h, d) for k in (1, nz - 1))
     twin = (z * 2 + (1 - h), d)
     pair = (e, (d + ndp // 2) % ndp)
 
-    barrier = pltpu.get_barrier_semaphore()
-    for device in (to[0], to[1], twin, pair):
-        pl.semaphore_signal(barrier, inc=1, device_id=device, device_id_type=MESH)
-    pl.semaphore_wait(barrier, 4)
+    def near_peer(k):
+        return (e, dx * near + (dy + k) % near)
+
+    def far_peer(k):
+        return (e, ((dx + k) % far) * near + dy)
 
     def remote(src, dst, send, recv, device):
         return pltpu.make_async_remote_copy(
@@ -83,6 +106,24 @@
             return contract(x_ref[block(index), :], up_ref[:, cols], 1, 0)
         return contract(rows_ref[block(index), :], down_ref[cols, :], 1, 1)
 
+    barrier = pltpu.get_barrier_semaphore()
+
+    def greet(device):
+        pl.semaphore_signal(barrier, inc=1, device_id=device, device_id_type=MESH)
+
+    for device in (to[0], to[1], twin):
+        greet(device)
+    for k in range(1, far):
+        greet(far_peer(k))
+
+    def greet_near(k, carry):
+        greet(near_peer(k))
+        return carry
+
+    lax.fori_loop(1, near, greet_near, 0)
+
+    forward = [(a, way) for a in (GATE, UP) for way in (0, 1)]
+
     def ring_copy(a, way, s):
         return remote(
             ring.at[a, way, s], ring.at[a, way, s + 1], ring_send.at[a, way, s], ring_recv.at[a, way, s], to[way]
@@ -91,33 +132,113 @@
     def chunk(way, s):
         return (z + (nz - 1 - s if way == 0 else 1 + s)) % nz
 
-    everything = [(a, way) for a in (GATE, UP, ACT) for way in (0, 1)]
-    for a, way in everything:
+    for a, way in forward:
         ring[a, way, 0] = term(a, way, chunk(way, 0)).astype(jnp.bfloat16)
+    pl.semaphore_wait(barrier, near + far + 1)
+    for a, way in forward:
         ring_copy(a, way, 0).start()
-    x_copy = remote(x_ref, x_other, x_send, x_recv, pair)
-    x_copy.start()
+
+    def near_copy(k):
+        peer = near_peer(k)
+        return remote(placed_ref.at[(dy + k) % near], mid.at[dy], near_send, near_recv, peer)
+
+    def near_start(k, carry):
+        near_copy(k).start()
+        return carry
+
+    lax.fori_loop(1, near, near_start, 0)
+    keep = pltpu.make_async_copy(placed_ref.at[dy], mid.at[dy], local_sem.at[0])
+    keep.start()
 
     def ring_step(s, carry):
-        for a, way in everything:
+        for a, way in forward:
             mine = term(a, way, chunk(way, s + 1))
             ring_copy(a, way, s).wait_recv()
             ring[a, way, s + 1] = (ring[a, way, s + 1].astype(jnp.float32) + mine).astype(jnp.bfloat16)
             ring_copy(a, way, s + 1).start()
         return carry
 
-    lax.fori_loop(0, nz - 2, ring_step, 0)
+    lax.fori_loop(0, FIRST, ring_step, 0)
+
+    near_all = remote(
+        placed_ref.at[pl.ds(0, near - 1)], mid.at[pl.ds(0, near - 1)], near_send, near_recv, near_peer(1)
+    )
+    near_all.wait_recv()
+    keep.wait()
+    far_copies = [
+        remote(mid.at[:, (dx + k) % far], arrived.at[dx], far_send.at[k], far_recv.at[k], far_peer(k))
+        for k in range(1, far)
+    ]
+    for copy in far_copies:
+        copy.start()
+    keep = pltpu.make_async_copy(mid.at[:, dx], arrived.at[dx], local_sem.at[1])
+    keep.start()
+    x_copy = remote(x_ref, x_other, x_send, x_recv, pair)
+    x_copy.start()
+
+    lax.fori_loop(FIRST, SECOND, ring_step, 0)
+
+    for copy in far_copies:
+        copy.wait_recv()
+    keep.wait()
+    rows_ref[...] = arrived[...].astype(jnp.float32).reshape(rows_ref.shape).astype(jnp.bfloat16)
+
+    reach = (nz // 2 - 1, nz // 2)
+
+    def act_copy(way, part, s):
+        return remote(
+            ring_act.at[way, part, s],
+            ring_act.at[way, part, s + 1],
+            act_send.at[way, part, s],
+            act_recv.at[way, part, s],
+            to[way],
+        )
+
+    def act_chunk(way, s):
+        return (z + (reach[0] - s if way == 0 else nz - reach[1] + s)) % nz
+
+    def act_step(s):
+        for part in (0, 1):
+            for way in (1, 0):
+                if s + 1 < reach[way]:
+                    mine = term(ACT, part, act_chunk(way, s + 1))
+                    act_copy(way, part, s).wait_recv()
+                    ring_act[way, part, s + 1] = (
+                        ring_act[way, part, s + 1].astype(jnp.float32) + mine
+                    ).astype(jnp.bfloat16)
+                    act_copy(way, part, s + 1).start()
+
+    for part in (0, 1):
+        for way in (1, 0):
+            ring_act[way, part, 0] = term(ACT, part, act_chunk(way, 0)).astype(jnp.bfloat16)
+            act_copy(way, part, 0).start()
 
     def swap_copy(a, way):
         return remote(swap_out.at[a, way], swap_in.at[a, way], swap_send.at[a, way], swap_recv.at[a, way], twin)
 
-    for a, way in everything:
-        mine = term(a, way, z)
-        ring_copy(a, way, nz - 2).wait_recv()
-        total = ring[a, way, nz - 1].astype(jnp.float32) + mine
+    def swap_start(a, way, total):
         own[a, way] = total
         swap_out[a, way] = total.astype(jnp.bfloat16)
         swap_copy(a, way).start()
+
+    act_done = 0
+    for s in range(SECOND, nz - 2):
+        ring_step(s, 0)
+        if act_done < reach[1] - 1:
+            act_step(act_done)
+            act_done += 1
+    for a, way in forward:
+        mine = term(a, way, z)
+        ring_copy(a, way, nz - 2).wait_recv()
+        swap_start(a, way, ring[a, way, nz - 1].astype(jnp.float32) + mine)
+    for s in range(act_done, reach[1] - 1):
+        act_step(s)
+    for part in (0, 1):
+        total = term(ACT, part, z)
+        for way in (0, 1):
+            act_copy(way, part, reach[way] - 1).wait_recv()
+            total = total + ring_act[way, part, reach[way]].astype(jnp.float32)
+        swap_start(ACT, part, total)
 
     def full_copy(a, way, s):
         at = block((z + (nz - s if way == 0 else s)) % nz)
@@ -174,23 +295,39 @@
             pair_copy(a, way).wait_recv()
             other_copy(a, way, 0).start()
 
+    for a in (GATE, UP):
+        for way in (0, 1):
+            full_copy(a, way, nz - 2).wait_recv()
+    going[...] = (
+        sum(
+            contract(full[a, way], w[:, pl.ds(way * half, half)], 1, 1)
+            for a, w in ((GATE, gate_ref), (UP, up_ref))
+            for way in (0, 1)
+        )
+        .reshape(going.shape)
+        .astype(jnp.bfloat16)
+    )
+    back_far = [
+        remote(
+            going.at[(dx + k) % far], mid_back.at[dx], back_far_send.at[k], back_far_recv.at[k], far_peer(k)
+        )
+        for k in range(1, far)
+    ]
+    for copy in back_far:
+        copy.start()
+    keep = pltpu.make_async_copy(going.at[dx], mid_back.at[dx], local_sem.at[2])
+    keep.start()
+
     down_copy = [
         remote(down_out.at[way], down_in.at[way], down_send.at[way], down_recv.at[way], pair) for way in (0, 1)
     ]
-    for way in (0, 1):
+
+    def down_part(way):
         full_copy(ACT, way, nz - 2).wait_recv()
         part = contract(full[ACT, way], rows_ref[...], 0, 0)
         grad_down_ref[pl.ds(way * half, half), :] = part.astype(jnp.bfloat16)
         down_out[way] = part.astype(jnp.bfloat16)
         down_copy[way].start()
-    for a in (GATE, UP):
-        for way in (0, 1):
-            full_copy(a, way, nz - 2).wait_recv()
-    returned_ref[...] = sum(
-        contract(full[a, way], w[:, pl.ds(way * half, half)], 1, 1)
-        for a, w in ((GATE, gate_ref), (UP, up_ref))
-        for way in (0, 1)
-    ).astype(jnp.bfloat16)
 
     def other_step(s, carry):
         for a in (GATE, UP):
@@ -199,7 +336,29 @@
                 other_copy(a, way, s + 1).start()
         return carry
 
-    lax.fori_loop(0, nz - 2, other_step, 0)
+    other_step(0, 0)
+    down_part(0)
+    other_step(1, 0)
+    down_part(1)
+    lax.fori_loop(2, 4, other_step, 0)
+
+    for copy in back_far:
+        copy.wait_recv()
+    keep.wait()
+
+    def back_copy(k):
+        return remote(
+            mid_back.at[:, (dy + k) % near], back.at[dy], back_near_send, back_near_recv, near_peer(k)
+        )
+
+    def back_start(k, carry):
+        back_copy(k).start()
+        return carry
+
+    lax.fori_loop(1, near, back_start, 0)
+    keep = pltpu.make_async_copy(mid_back.at[:, dy], back.at[dy], local_sem.at[3])
+    keep.start()
+    lax.fori_loop(4, nz - 2, other_step, 0)
 
     x_copy.wait_recv()
     shared = shared_ref[0:1, 0:1]
@@ -209,6 +368,15 @@
             other_copy(a, way, nz - 2).wait_recv()
             part = part + shared * contract(x_other[...], other[a, way], 0, 0)
             out[:, pl.ds(way * half, half)] = part.astype(jnp.bfloat16)
+
+    everything_back = remote(
+        back.at[pl.ds(0, near - 1)], back.at[pl.ds(0, near - 1)], back_near_send, back_near_recv, near_peer(1)
+    )
+    everything_back.wait_recv()
+    keep.wait()
+    came = back[...].astype(jnp.float32).reshape(rows_ref.shape).astype(jnp.bfloat16)
+    grad_input_ref[...] = contract(pick_ref[...], came, 1, 0).astype(jnp.bfloat16)
+
     for way in (0, 1):
         at = pl.ds(way * half, half)
         down_copy[way].wait_recv()
@@ -216,6 +384,10 @@
             grad_down_ref[at, :].astype(jnp.float32) + shared * down_in[way].astype(jnp.float32)
         ).astype(jnp.bfloat16)
 
+    near_all.wait_send()
+    everything_back.wait_send()
+    for copy in far_copies + back_far:
+        copy.wait_send()
     x_copy.wait_send()
     for way in (0, 1):
         down_copy[way].wait_send()
@@ -223,39 +395,51 @@
             swap_copy(a, way).wait_send()
         for a in (GATE, UP):
             pair_copy(a, way).wait_send()
+        for part in (0, 1):
+            for s in range(reach[way]):
+                act_copy(way, part, s).wait_send()
 
     def drain(s, carry):
-        for a, way in everything:
-            ring_copy(a, way, s).wait_send()
-            full_copy(a, way, s).wait_send()
-            if a != ACT:
+        for way in (0, 1):
+            for a in (GATE, UP):
+                ring_copy(a, way, s).wait_send()
                 other_copy(a, way, s).wait_send()
+            for a in (GATE, UP, ACT):
+                full_copy(a, way, s).wait_send()
         return carry
 
     lax.fori_loop(0, nz - 1, drain, 0)
 
 
-def slot_call(shared, x, rows, gate_w, up_w, down_w):
+def slot_call(shared, x, placed, pick, gate_w, up_w, down_w):
     nz = lax.axis_size("expert") // 2
     count, width = x.shape
     hidden = gate_w.shape[1]
     half = hidden // 2
     part = count // nz
+    near, far, capacity, _ = placed.shape
     bf16, f32 = jnp.bfloat16, jnp.float32
     vmem = pl.BlockSpec(memory_space=pltpu.VMEM)
     dma = pltpu.SemaphoreType.DMA
     return pl.pallas_call(
         slot_kernel,
         out_shape=(
-            jax.ShapeDtypeStruct((count, width), bf16),
+            jax.ShapeDtypeStruct((pick.shape[0], width), bf16),
             jax.ShapeDtypeStruct((width, hidden), bf16),
             jax.ShapeDtypeStruct((width, hidden), bf16),
             jax.ShapeDtypeStruct((hidden, width), bf16),
         ),
-        in_specs=[vmem] * 6,
+        in_specs=[vmem] * 7,
         out_specs=(vmem,) * 4,
         scratch_shapes=[
-            pltpu.VMEM((3, 2, nz, part, half), bf16),
+            pltpu.VMEM((near, far, capacity, width), bf16),
+            pltpu.VMEM((far, near, capacity, width), bf16),
+            pltpu.VMEM((count, width), bf16),
+            pltpu.VMEM((far, near, capacity, width), bf16),
+            pltpu.VMEM((far, near, capacity, width), bf16),
+            pltpu.VMEM((near, far, capacity, width), bf16),
+            pltpu.VMEM((2, 2, nz, part, half), bf16),
+            pltpu.VMEM((2, 2, nz // 2 + 1, part, half), bf16),
             pltpu.VMEM((3, 2, part, half), f32),
             pltpu.VMEM((3, 2, part, half), bf16),
             pltpu.VMEM((3, 2, part, half), bf16),
@@ -264,8 +448,19 @@
             pltpu.VMEM((count, width), bf16),
             pltpu.VMEM((2, half, width), bf16),
             pltpu.VMEM((2, half, width), bf16),
-            dma((3, 2, nz - 1)),
-            dma((3, 2, nz - 1)),
+            dma,
+            dma,
+            dma((far,)),
+            dma((far,)),
+            dma((far,)),
+            dma((far,)),
+            dma,
+            dma,
+            dma((4,)),
+            dma((2, 2, nz - 1)),
+            dma((2, 2, nz - 1)),
+            dma((2, 2, nz // 2)),
+            dma((2, 2, nz // 2)),
             dma((3, 2)),
             dma((3, 2)),
             dma((3, 2, nz - 1)),
@@ -282,7 +477,7 @@
         compiler_params=pltpu.CompilerParams(
             collective_id=0, has_side_effects=True, vmem_limit_bytes=40 * 1024 * 1024
         ),
-    )(shared, x, rows, gate_w, up_w, down_w)
+    )(shared, x, placed, pick, gate_w, up_w, down_w)
 
 
 def local(
@@ -292,47 +487,35 @@
     fanout = routes.shape[1]
     slot_count = lax.axis_size("dp")
     capacity = saved_input.shape[1] // slot_count
+    far = FAR
+    near = slot_count // far
     flat_routes = routes.reshape(-1)
     chosen = (flat_routes[:, None] == jnp.arange(slot_count, dtype=jnp.int32)[None, :]).astype(
         jnp.int32
     )
     earlier = jnp.cumsum(chosen, axis=0) - chosen
     position = jnp.sum(earlier * chosen, axis=1)
-    target = flat_routes * capacity + position
-    select = (
-        jnp.arange(slot_count * capacity, dtype=jnp.int32)[:, None] == target[None, :]
+    target = ((flat_routes % near) * far + flat_routes // near) * capacity + position
+    slots = jnp.arange(slot_count * capacity, dtype=jnp.int32)
+    select = (slots[:, None] == target[None, :]).astype(jnp.bfloat16)
+    pick = jnp.sum(
+        (target.reshape(tok_rows, fanout, 1) == slots[None, None, :]).astype(jnp.float32), axis=1
     ).astype(jnp.bfloat16)
     scaled = (gate_prob[:, :, None] * grad_out[:, None, :].astype(jnp.float32)).astype(jnp.bfloat16)
     scaled = scaled.reshape(tok_rows * fanout, width_part)
     placed = jnp.dot(select, scaled, preferred_element_type=jnp.float32).astype(jnp.bfloat16)
-    arrived = lax.all_to_all(
-        placed.reshape(slot_count, capacity, width_part),
-        "dp",
-        split_axis=0,
-        concat_axis=0,
-        tiled=True,
-    )
-    grad_rows = arrived.reshape(slot_count * capacity, width_part)
     my_slot = lax.axis_index("dp")
     partner = (my_slot + slot_count // 2) % slot_count
     shared = (slot_expert[my_slot] == slot_expert[partner]).astype(jnp.float32)
-    returned, grad_gate_w, grad_up_w, grad_down_w = slot_call(
+    grad_input, grad_gate_w, grad_up_w, grad_down_w = slot_call(
         jnp.full((8, 128), shared, jnp.float32),
         saved_input[0],
-        grad_rows,
+        placed.reshape(near, far, capacity, width_part),
+        pick,
         gate_weight[0],
         up_weight[0],
         down_weight[0],
     )
-    back = lax.all_to_all(
-        returned.reshape(slot_count, capacity, width_part),
-        "dp",
-        split_axis=0,
-        concat_axis=0,
-        tiled=True,
-    )
-    picked = contract(select, back.reshape(slot_count * capacity, width_part), 0, 0)
-    grad_input = jnp.sum(picked.reshape(tok_rows, fanout, width_part), axis=1).astype(jnp.bfloat16)
     return (grad_input, grad_gate_w[None], grad_up_w[None], grad_down_w[None])
 
 

time: 179 us -> 149 us (0.83)
  the two profiles are of different devices: /device:TPU:1 before, /device:TPU:18 now
where the time goes in v2:
time: 149 us; the launch traced here: 148 us
  Pallas kernels  137 us (92%)
  local copies, waits for them, and re-layouts  7.57 us (5%)
  between operations  2.06 us (1%)
  other arithmetic  1.77 us (1%)
    pallas_call x1, Pallas kernels, slot_call(): pl.pallas_call(slot_kernel, out_shape=(jax.ShapeDtypeStruct((pick.shape[0...  137 us
    unnamed x18, local copies, waits for them, and re-layouts  6.45 us

profile of v2, /device:TPU:18, one launch (start us, length us, event | category | flops | bytes accessed | tf_op | source)
XLA Modules:
  0.0 148.2 jit_solution(7798374644498777323)
XLA Ops:
  0.6 0.0 copy-start.4
  0.6 0.0 copy-start.5
  0.7 0.0 copy-start.1
  0.7 0.0 copy-start
  0.7 0.6 copy-done.5
  1.3 0.6 fusion.19
  3.2 0.0 copy-done.4
  3.2 0.1 copy.21
  3.3 0.1 reshape.130
  3.4 0.1 eq.62
  3.5 0.8 copy.24
  4.2 0.1 mul.58
  4.3 0.7 convert_element_type.35
  5.1 0.6 reduce-window.6
  5.7 0.2 slice_reduce_fusion
  5.9 0.1 fusion.7
  6.0 0.1 reduce_sum.21
  6.2 0.2 convert_reduce_fusion.pick_ref
  6.4 0.3 convolution_convert_fusion
  6.7 0.0 copy-done.1
  6.7 0.0 copy-done
  6.7 0.0 copy-start.2
  6.7 1.0 copy-done.2
  7.8 0.0 copy-start.3
  7.8 0.9 copy-done.3
  8.7 136.5 %shard_map.111 = (bf16[32,256]{1,0:T(8,128)(2,1)S(1)}, bf16[256,1024]{1,0:T(8,128)(2,1)S(1)}, bf16[256,1024]{1,0:T(8,128)(2,1)S(1)}, bf16[1024,256]{1,0:T(8,128)(2,1)S(1)}) custom-call(f32[8,128]{1,0:T(8,128)S(1)} %broadcast_in_dim.8.shared_ref, bf16[512,256]{1,0:T(8,128)(2,1)S(1)} %bitcast.39, bf16[16,4,8,256]{3,2,1,0:T(8,128)(2,1)S(1)} %bitcast.40, ...), custom_call_target="tpu_custom_call" | custom-call | tf_op jit(solution)/shard_map/pallas_call | solution.py:424
  145.3 0.6 copy.35
  145.9 0.8 copy.36
  146.7 0.8 copy.37
  147.4 0.8 copy.38
  (6 shorter events, 0.1 us)
Async XLA Ops:
  0.6 2.6 %copy-start.4 = (s32[32,8]{0,1:T(8,128)S(1)}, s32[32,8]{0,1:T(8,128)}, u32[]{:S(2)}) copy-start(s32[32,8]{0,1:T(8,128)} %param.10) | copy-start | bytes 3076
  0.6 0.7 copy-start.5
  0.7 6.0 %copy-start.1 = (bf16[1,256,1024]{2,1,0:T(8,128)(2,1)S(1)}, bf16[1,256,1024]{2,1,0:T(8,128)(2,1)}, u32[]{:S(2)}) copy-start(bf16[1,256,1024]{2,1,0:T(8,128)(2,1)} %param.14) | copy-start | bytes 1572868
  0.7 6.0 %copy-start = (bf16[1,256,1024]{2,1,0:T(8,128)(2,1)S(1)}, bf16[1,256,1024]{2,1,0:T(8,128)(2,1)}, u32[]{:S(2)}) copy-start(bf16[1,256,1024]{2,1,0:T(8,128)(2,1)} %param.13) | copy-start | bytes 1572868
  6.7 1.0 copy-start.2
  7.8 0.9 copy-start.3

commit v3 on v2

v3 whole, which is shorter than its diff:
```python
import jax
import jax.numpy as jnp
from jax import lax
from jax.experimental import pallas as pl
from jax.experimental.pallas import tpu as pltpu
from jax.sharding import PartitionSpec as P

MESH = pl.DeviceIdType.MESH
GATE, UP, ACT = 0, 1, 2
OTHER = 3
FAR = 4


def contract(left, right, left_dim, right_dim):
    return lax.dot_general(
        left, right, (((left_dim,), (right_dim,)), ((), ())), preferred_element_type=jnp.float32
    )


def slot_kernel(
    routes_ref,
    prob_ref,
    grad_out_ref,
    expert_ref,
    x_hbm,
    gate_hbm,
    up_hbm,
    down_hbm,
    grad_input_ref,
    grad_gate_ref,
    grad_up_ref,
    grad_down_ref,
    x_ref,
    gate_ref,
    up_ref,
    down_ref,
    pick_ref,
    placed_ref,
    mid,
    arrived,
    rows_ref,
    going,
    mid_back,
    back,
    ring,
    own,
    swap_out,
    swap_in,
    full,
    other,
    x_other,
    x_turned,
    part_own,
    down_out,
    down_in,
    load_sem,
    near_send,
    near_recv,
    far_send,
    far_recv,
    back_far_send,
    back_far_recv,
    back_near_send,
    back_near_recv,
    local_sem,
    ring_send,
    ring_recv,
    swap_send,
    swap_recv,
    full_send,
    full_recv,
    pair_send,
    pair_recv,
    x_send,
    x_recv,
    down_send,
    down_recv,
):
    e = lax.axis_index("expert")
    d = lax.axis_index("dp")
    nz = lax.axis_size("expert") // 2
    ndp = lax.axis_size("dp")
    far, near = mid.shape[1], mid.shape[0]
    dx, dy = d // near, d % near
    z, h = e // 2, e % 2
    rows = x_ref.shape[0] // nz
    half = gate_ref.shape[1] // 2
    to = tuple((((z + k) % nz) * 2 + h, d) for k in (1, nz - 1))
    twin = (z * 2 + (1 - h), d)
    pair = (e, (d + ndp // 2) % ndp)

    def near_peer(k):
        return (e, dx * near + (dy + k) % near)

    def far_peer(k):
        return (e, ((dx + k) % far) * near + dy)

    def remote(src, dst, send, recv, device):
        return pltpu.make_async_remote_copy(
            src_ref=src, dst_ref=dst, send_sem=send, recv_sem=recv, device_id=device, device_id_type=MESH
        )

    def block(index):
        return pl.ds(pl.multiple_of(index * rows, rows), rows)

    def term(a, way, index):
        cols = pl.ds(way * half, half)
        if a == GATE:
            return contract(x_ref[block(index), :], gate_ref[:, cols], 1, 0)
        if a == UP:
            return contract(x_ref[block(index), :], up_ref[:, cols], 1, 0)
        return contract(rows_ref[block(index), :], down_ref[cols, :], 1, 1)

    loads = [
        pltpu.make_async_copy(src, dst, load_sem.at[i])
        for i, (src, dst) in enumerate(
            ((x_hbm, x_ref), (gate_hbm, gate_ref), (up_hbm, up_ref), (down_hbm, down_ref))
        )
    ]
    for load in loads:
        load.start()

    barrier = pltpu.get_barrier_semaphore()

    def greet(device):
        pl.semaphore_signal(barrier, inc=1, device_id=device, device_id_type=MESH)

    for device in (to[0], to[1], twin):
        greet(device)
    for k in range(1, far):
        greet(far_peer(k))

    def greet_near(k, carry):
        greet(near_peer(k))
        return carry

    lax.fori_loop(1, near, greet_near, 0)

    capacity = placed_ref.shape[2]
    shape = (near * far * capacity, routes_ref.shape[1])
    line = lax.broadcasted_iota(jnp.int32, shape, 0)
    group = lax.div(line, capacity)
    slot = lax.rem(group, far) * near + lax.div(group, far)
    chosen = jnp.zeros(shape, jnp.float32)
    weight = jnp.zeros(shape, jnp.float32)
    for k in range(routes_ref.shape[0]):
        same = routes_ref[k : k + 1, :] == slot
        chosen = jnp.where(same, 1.0, chosen)
        weight = jnp.where(same, prob_ref[k : k + 1, :], weight)
    tokens = (shape[1], shape[1])
    before = jnp.where(
        lax.broadcasted_iota(jnp.int32, tokens, 0) < lax.broadcasted_iota(jnp.int32, tokens, 1), 1.0, 0.0
    ).astype(jnp.bfloat16)
    earlier = contract(chosen.astype(jnp.bfloat16), before, 1, 0)
    pick = jnp.where(earlier == lax.rem(line, capacity).astype(jnp.float32), chosen, 0.0)
    pick_ref[...] = pick.astype(jnp.bfloat16)
    scale = jnp.sum(pick * weight, axis=1, keepdims=True)
    placed = scale * contract(pick.astype(jnp.bfloat16), grad_out_ref[...], 1, 0)
    placed_ref[...] = placed.reshape(placed_ref.shape).astype(jnp.bfloat16)

    reach = nz // 2

    def ring_copy(a, way, part, s):
        return remote(
            ring.at[a, way, part, s],
            ring.at[a, way, part, s + 1],
            ring_send.at[a, way, part, s],
            ring_recv.at[a, way, part, s],
            to[way],
        )

    def ring_term(a, way, part, s):
        return term(a, part, (z + (reach - s if way == 0 else nz - reach + s)) % nz)

    def ring_start(a, way):
        for part, s in ((way, 0), (1 - way, 1)):
            ring[a, way, part, s] = ring_term(a, way, part, s).astype(jnp.bfloat16)

    def ring_send_first(a, way):
        for part, s in ((way, 0), (1 - way, 1)):
            ring_copy(a, way, part, s).start()

    def ring_step(a, i):
        for ahead in (0, 1):
            s = i + ahead
            if s + 1 < reach:
                for way in (0, 1):
                    part = way if ahead == 0 else 1 - way
                    mine = ring_term(a, way, part, s + 1)
                    ring_copy(a, way, part, s).wait_recv()
                    ring[a, way, part, s + 1] = (
                        ring[a, way, part, s + 1].astype(jnp.float32) + mine
                    ).astype(jnp.bfloat16)
                    ring_copy(a, way, part, s + 1).start()

    def ring_end(a):
        for part in (0, 1):
            total = term(a, part, z)
            for way in (0, 1):
                ring_copy(a, way, part, reach - 1).wait_recv()
                total = total + ring[a, way, part, reach].astype(jnp.float32)
            own[a, part] = total
            swap_out[a, part] = total.astype(jnp.bfloat16)
            swap_copy(a, part).start()

    def swap_copy(a, way):
        return remote(swap_out.at[a, way], swap_in.at[a, way], swap_send.at[a, way], swap_recv.at[a, way], twin)

    for load in loads[:3]:
        load.wait()
    for a in (GATE, UP):
        for way in (0, 1):
            ring_start(a, way)
    pl.semaphore_wait(barrier, near + far + 1)

    def near_copy(k):
        peer = near_peer(k)
        return remote(placed_ref.at[(dy + k) % near], mid.at[dy], near_send, near_recv, peer)

    def near_start(k, carry):
        near_copy(k).start()
        return carry

    lax.fori_loop(1, near, near_start, 0)
    for a in (GATE, UP):
        for way in (0, 1):
            ring_send_first(a, way)
    keep = pltpu.make_async_copy(placed_ref.at[dy], mid.at[dy], local_sem.at[0])
    keep.start()

    ring_step(GATE, 0)
    ring_step(UP, 0)

    near_all = remote(
        placed_ref.at[pl.ds(0, near - 1)], mid.at[pl.ds(0, near - 1)], near_send, near_recv, near_peer(1)
    )
    near_all.wait_recv()
    keep.wait()
    far_copies = [
        remote(mid.at[:, (dx + k) % far], arrived.at[dx], far_send.at[k], far_recv.at[k], far_peer(k))
        for k in range(1, far)
    ]
    for copy in far_copies:
        copy.start()
    keep = pltpu.make_async_copy(mid.at[:, dx], arrived.at[dx], local_sem.at[1])
    keep.start()

    ring_step(GATE, 1)
    ring_step(UP, 1)

    for copy in far_copies:
        copy.wait_recv()
    keep.wait()
    loads[3].wait()
    rows_ref[...] = arrived[...].astype(jnp.float32).reshape(rows_ref.shape).astype(jnp.bfloat16)

    for way in (0, 1):
        ring_start(ACT, way)
        ring_send_first(ACT, way)
    ring_step(GATE, 2)
    ring_step(UP, 2)
    ring_step(ACT, 0)
    ring_end(GATE)
    ring_end(UP)
    ring_step(ACT, 1)
    ring_step(ACT, 2)
    ring_end(ACT)

    def gather_copy(a, way, part, s):
        at = block((z + (nz - s if way == 0 else s)) % nz)
        array = full.at[a, part, at, :] if a < 3 else other.at[a - 3, part, at, :]
        return remote(array, array, full_send.at[a, way, part, s], full_recv.at[a, way, part, s], to[way])

    def gather_start(a, part):
        for way in (0, 1):
            gather_copy(a, way, part, 0).start()

    def gather_step(a, s):
        for part in (0, 1):
            for way in (0, 1):
                gather_copy(a, way, part, s).wait_recv()
                if s + 2 < reach or way == part:
                    gather_copy(a, way, part, s + 1).start()

    def gather_end(a, part):
        gather_copy(a, part, part, reach - 1).wait_recv()

    def pair_copy(a, way):
        at = block(z)
        return remote(
            full.at[a, way, at, :], other.at[a, way, at, :], pair_send.at[a, way], pair_recv.at[a, way], pair
        )

    for way in (0, 1):
        value = []
        for a in (GATE, UP, ACT):
            swap_copy(a, way).wait_recv()
            value.append(own[a, way] + swap_in[a, way].astype(jnp.float32))
        gate_pre, up_pre, grad_act = value
        sigmoid_gate = jax.nn.sigmoid(gate_pre)
        gated = gate_pre * sigmoid_gate
        full[ACT, way, block(z), :] = (gated * up_pre).astype(jnp.bfloat16)
        gather_start(ACT, way)
        full[GATE, way, block(z), :] = (
            grad_act * up_pre * sigmoid_gate * (1.0 + gate_pre * (1.0 - sigmoid_gate))
        ).astype(jnp.bfloat16)
        gather_start(GATE, way)
        full[UP, way, block(z), :] = (grad_act * gated).astype(jnp.bfloat16)
    for way in (0, 1):
        pair_copy(GATE, way).start()
        pair_copy(UP, way).start()
    x_copy = remote(x_ref, x_other, x_send, x_recv, pair)
    x_copy.start()
    x_turned[...] = x_ref[...].T

    def down_part(way):
        gather_end(ACT, way)
        part = contract(full[ACT, way], rows_ref[...], 0, 0)
        grad_down_ref[pl.ds(way * half, half), :] = part.astype(jnp.bfloat16)
        down_out[way] = part.astype(jnp.bfloat16)
        down_copy[way].start()

    down_copy = [
        remote(down_out.at[way], down_in.at[way], down_send.at[way], down_recv.at[way], pair) for way in (0, 1)
    ]
    gather_step(ACT, 0)
    gather_step(GATE, 0)
    for part in (0, 1):
        gather_start(UP, part)
    gather_step(ACT, 1)
    gather_step(GATE, 1)
    gather_step(UP, 0)
    gather_step(ACT, 2)
    gather_step(GATE, 2)
    gather_step(UP, 1)
    for a in (GATE, UP):
        for part in (0, 1):
            pair_copy(a, part).wait_recv()
            gather_start(OTHER + a, part)
    down_part(0)
    gather_step(UP, 2)
    down_part(1)
    gather_step(OTHER + GATE, 0)
    gather_step(OTHER + UP, 0)
    for a in (GATE, UP):
        for part in (0, 1):
            gather_end(a, part)
    going[...] = (
        sum(
            contract(full[a, way], w[:, pl.ds(way * half, half)], 1, 1)
            for a, w in ((GATE, gate_ref), (UP, up_ref))
            for way in (0, 1)
        )
        .reshape(going.shape)
        .astype(jnp.bfloat16)
    )
    back_far = [
        remote(
            going.at[(dx + k) % far], mid_back.at[dx], back_far_send.at[k], back_far_recv.at[k], far_peer(k)
        )
        for k in range(1, far)
    ]
    for copy in back_far:
        copy.start()
    keep = pltpu.make_async_copy(going.at[dx], mid_back.at[dx], local_sem.at[2])
    keep.start()

    def own_part(a, way):
        part_own[a, way] = contract(x_turned[...], full[a, way], 1, 0)

    gather_step(OTHER + GATE, 1)
    own_part(GATE, 0)
    gather_step(OTHER + UP, 1)
    own_part(GATE, 1)
    for copy in back_far:
        copy.wait_recv()
    keep.wait()

    def back_copy(k):
        return remote(
            mid_back.at[:, (dy + k) % near], back.at[dy], back_near_send, back_near_recv, near_peer(k)
        )

    def back_start(k, carry):
        back_copy(k).start()
        return carry

    lax.fori_loop(1, near, back_start, 0)
    keep = pltpu.make_async_copy(mid_back.at[:, dy], back.at[dy], local_sem.at[3])
    keep.start()
    gather_step(OTHER + GATE, 2)
    own_part(UP, 0)
    gather_step(OTHER + UP, 2)
    own_part(UP, 1)
    x_copy.wait_recv()
    x_turned[...] = x_other[...].T
    d_line = lax.broadcasted_iota(jnp.int32, expert_ref.shape, 1)
    mine = jnp.sum(jnp.where(d_line == d, expert_ref[...], 0), axis=1, keepdims=True)
    theirs = jnp.sum(jnp.where(d_line == pair[1], expert_ref[...], 0), axis=1, keepdims=True)
    shared = jnp.where(mine == theirs, 1.0, 0.0)
    for a, out in ((GATE, grad_gate_ref), (UP, grad_up_ref)):
        for way in (0, 1):
            gather_end(OTHER + a, way)
            part = part_own[a, way] + shared * contract(x_turned[...], other[a, way], 1, 0)
            out[:, pl.ds(way * half, half)] = part.astype(jnp.bfloat16)

    everything_back = remote(
        back.at[pl.ds(0, near - 1)], back.at[pl.ds(0, near - 1)], back_near_send, back_near_recv, near_peer(1)
    )
    everything_back.wait_recv()
    keep.wait()
    came = back[...].astype(jnp.float32).reshape(rows_ref.shape).astype(jnp.bfloat16)
    grad_input_ref[...] = contract(pick_ref[...], came, 0, 0).astype(jnp.bfloat16)

    for way in (0, 1):
        at = pl.ds(way * half, half)
        down_copy[way].wait_recv()
        grad_down_ref[at, :] = (
            grad_down_ref[at, :].astype(jnp.float32) + shared * down_in[way].astype(jnp.float32)
        ).astype(jnp.bfloat16)

    near_all.wait_send()
    everything_back.wait_send()
    for copy in far_copies + back_far:
        copy.wait_send()
    x_copy.wait_send()
    for way in (0, 1):
        down_copy[way].wait_send()
        for a in (GATE, UP, ACT):
            swap_copy(a, way).wait_send()
        for a in (GATE, UP):
            pair_copy(a, way).wait_send()

    def drain(part, carry):
        for way in (0, 1):
            for a in range(5):
                for step in range(reach - 1):
                    gather_copy(a, way, part, step).wait_send()
            for a in (GATE, UP, ACT):
                for step in range(1, reach):
                    ring_copy(a, way, part, step).wait_send()
        for a in range(5):
            gather_copy(a, part, part, reach - 1).wait_send()
        for a in (GATE, UP, ACT):
            ring_copy(a, part, part, 0).wait_send()
        return carry

    for part in (0, 1):
        drain(part, 0)


def slot_call(routes, prob, grad_out, expert, x, gate_w, up_w, down_w):
    nz = lax.axis_size("expert") // 2
    count, width = x.shape
    hidden = gate_w.shape[1]
    half = hidden // 2
    part = count // nz
    far = FAR
    near = lax.axis_size("dp") // far
    capacity = count // (near * far)
    tokens = grad_out.shape[0]
    bf16, f32 = jnp.bfloat16, jnp.float32
    vmem = pl.BlockSpec(memory_space=pltpu.VMEM)
    hbm = pl.BlockSpec(memory_space=pl.ANY)
    dma = pltpu.SemaphoreType.DMA
    return pl.pallas_call(
        slot_kernel,
        out_shape=(
            jax.ShapeDtypeStruct((tokens, width), bf16),
            jax.ShapeDtypeStruct((width, hidden), bf16),
            jax.ShapeDtypeStruct((width, hidden), bf16),
            jax.ShapeDtypeStruct((hidden, width), bf16),
        ),
        in_specs=[vmem] * 4 + [hbm] * 4,
        out_specs=(vmem,) * 4,
        scratch_shapes=[
            pltpu.VMEM((count, width), bf16),
            pltpu.VMEM((width, hidden), bf16),
            pltpu.VMEM((width, hidden), bf16),
            pltpu.VMEM((hidden, width), bf16),
            pltpu.VMEM((count, tokens), bf16),
            pltpu.VMEM((near, far, capacity, width), bf16),
            pltpu.VMEM((near, far, capacity, width), bf16),
            pltpu.VMEM((far, near, capacity, width), bf16),
            pltpu.VMEM((count, width), bf16),
            pltpu.VMEM((far, near, capacity, width), bf16),
            pltpu.VMEM((far, near, capacity, width), bf16),
            pltpu.VMEM((near, far, capacity, width), bf16),
            pltpu.VMEM((3, 2, 2, nz // 2 + 1, part, half), bf16),
            pltpu.VMEM((3, 2, part, half), f32),
            pltpu.VMEM((3, 2, part, half), bf16),
            pltpu.VMEM((3, 2, part, half), bf16),
            pltpu.VMEM((3, 2, count, half), bf16),
            pltpu.VMEM((2, 2, count, half), bf16),
            pltpu.VMEM((count, width), bf16),
            pltpu.VMEM((width, count), bf16),
            pltpu.VMEM((2, 2, width, half), f32),
            pltpu.VMEM((2, half, width), bf16),
            pltpu.VMEM((2, half, width), bf16),
            dma((4,)),
            dma,
            dma,
            dma((far,)),
            dma((far,)),
            dma((far,)),
            dma((far,)),
            dma,
            dma,
            dma((4,)),
            dma((3, 2, 2, nz // 2)),
            dma((3, 2, 2, nz // 2)),
            dma((3, 2)),
            dma((3, 2)),
            dma((5, 2, 2, nz // 2)),
            dma((5, 2, 2, nz // 2)),
            dma((2, 2)),
            dma((2, 2)),
            dma,
            dma,
            dma((2,)),
            dma((2,)),
        ],
        compiler_params=pltpu.CompilerParams(
            collective_id=0, has_side_effects=True, vmem_limit_bytes=56 * 1024 * 1024
        ),
    )(routes, prob, grad_out, expert, x, gate_w, up_w, down_w)


def local(
    grad_out, gate_prob, routes, slot_expert, saved_input, gate_weight, up_weight, down_weight
):
    grad_input, grad_gate_w, grad_up_w, grad_down_w = slot_call(
        routes.T,
        gate_prob.T,
        grad_out,
        slot_expert[None],
        saved_input[0],
        gate_weight[0],
        up_weight[0],
        down_weight[0],
    )
    return (grad_input, grad_gate_w[None], grad_up_w[None], grad_down_w[None])


def solution(mesh):
    placed = (
        P("dp", "expert"),
        P("dp", None),
        P("dp", None),
        P(),
        P("dp", None, "expert"),
        P("dp", "expert", None),
        P("dp", "expert", None),
        P("dp", None, "expert"),
    )
    return jax.shard_map(
        local,
        mesh=mesh,
        in_specs=placed,
        out_specs=(
            P("dp", "expert"),
            P("dp", "expert", None),
            P("dp", "expert", None),
            P("dp", None, "expert"),
        ),
        check_vma=False,
    )
```

time: 149 us -> 138 us (0.926)
  the two profiles are of different devices: /device:TPU:18 before, /device:TPU:1 now
where the time goes in v3:
time: 138 us
  Pallas kernels  132 us (96%)
  local copies, waits for them, and re-layouts  5.28 us (4%)
    pallas_call x1, Pallas kernels, slot_call(): pl.pallas_call(slot_kernel, out_shape=(jax.ShapeDtypeStruct((tokens, widt...  132 us
    unnamed x8, local copies, waits for them, and re-layouts  5.28 us

profile of v3, /device:TPU:1, one launch (start us, length us, event | category | flops | bytes accessed | tf_op | source)
XLA Modules:
  0.0 137.7 jit_solution(3165304501434929627)
XLA Ops:
  0.6 131.8 %shard_map.111 = (bf16[32,256]{1,0:T(8,128)(2,1)}, bf16[256,1024]{1,0:T(8,128)(2,1)}, bf16[256,1024]{1,0:T(8,128)(2,1)}, bf16[1024,256]{1,0:T(8,128)(2,1)}) custom-call(s32[8,32]{1,0:T(8,128)} %bitcast.17, f32[8,32]{1,0:T(8,128)} %bitcast.18, bf16[32,256]{1,0:T(8,128)(2,1)} %grad_out_ref.1, s32[1,64]{1,0:T(1,128)} %bitcast.19, bf16[512,256]{1,0:T(8,128)(2,1)} %bitcast.16, ...), custom_call_target="tpu_custom_call" | custom-call | tf_op jit(solution)/shard_map/pallas_call | solution.py:466
  132.4 1.3 copy.16
  133.7 0.0 copy-start.1
  133.7 1.9 %copy.17 = bf16[1,256,1024]{2,1,0:T(8,128)(2,1)} copy(bf16[1,256,1024]{2,1,0:T(8,128)(2,1)} %bitcast.12) | data formatting | bytes 1048576
  135.6 0.0 copy-done.1
  135.6 0.0 copy-start
  135.6 0.8 copy.18
  136.4 0.4 copy-done
  136.9 0.8 copy.19
Async XLA Ops:
  133.7 1.9 %copy-start.1 = (bf16[256,1024]{1,0:T(8,128)(2,1)S(1)}, bf16[256,1024]{1,0:T(8,128)(2,1)}, u32[]{:S(2)}) copy-start(bf16[256,1024]{1,0:T(8,128)(2,1)} %get-tuple-element.10) | copy-start | bytes 1572868
  135.6 1.2 copy-start

commit v4 on v3

--- a/solution.py
+++ b/solution.py
@@ -67,6 +67,8 @@
     ring_recv,
     swap_send,
     swap_recv,
+    twin_send,
+    twin_recv,
     full_send,
     full_recv,
     pair_send,
@@ -103,6 +105,11 @@
     def block(index):
         return pl.ds(pl.multiple_of(index * rows, rows), rows)
 
+    few = rows // 2
+
+    def lot(index):
+        return pl.ds(pl.multiple_of(index * few, few), few)
+
     def term(a, way, index):
         cols = pl.ds(way * half, half)
         if a == GATE:
@@ -204,7 +211,13 @@
             swap_copy(a, part).start()
 
     def swap_copy(a, way):
-        return remote(swap_out.at[a, way], swap_in.at[a, way], swap_send.at[a, way], swap_recv.at[a, way], twin)
+        return remote(
+            swap_out.at[a, way, lot(1 - h), :],
+            swap_in.at[a, way],
+            swap_send.at[a, way],
+            swap_recv.at[a, way],
+            twin,
+        )
 
     for load in loads[:3]:
         load.wait()
@@ -266,24 +279,35 @@
     ring_step(ACT, 2)
     ring_end(ACT)
 
-    def gather_copy(a, way, part, s):
-        at = block((z + (nz - s if way == 0 else s)) % nz)
+    def piece(s, which):
+        return lot(s % nz * 2 + (h if which == 0 else 1 - h))
+
+    def gather_copy(a, way, part, s, which):
+        at = piece(z + (nz - s if way == 0 else s), which)
         array = full.at[a, part, at, :] if a < 3 else other.at[a - 3, part, at, :]
-        return remote(array, array, full_send.at[a, way, part, s], full_recv.at[a, way, part, s], to[way])
-
-    def gather_start(a, part):
+        return remote(
+            array, array, full_send.at[a, which, way, part, s], full_recv.at[a, which, way, part, s], to[way]
+        )
+
+    def gather_start(a, part, which):
         for way in (0, 1):
-            gather_copy(a, way, part, 0).start()
+            gather_copy(a, way, part, 0, which).start()
 
     def gather_step(a, s):
-        for part in (0, 1):
-            for way in (0, 1):
-                gather_copy(a, way, part, s).wait_recv()
-                if s + 2 < reach or way == part:
-                    gather_copy(a, way, part, s + 1).start()
+        for which in (0, 1):
+            for part in (0, 1):
+                for way in (0, 1):
+                    gather_copy(a, way, part, s, which).wait_recv()
+                    if s + 2 < reach or way == part:
+                        gather_copy(a, way, part, s + 1, which).start()
 
     def gather_end(a, part):
-        gather_copy(a, part, part, reach - 1).wait_recv()
+        for which in (0, 1):
+            gather_copy(a, part, part, reach - 1, which).wait_recv()
+
+    def twin_copy(a, part):
+        array = full.at[a, part, piece(z, 0), :]
+        return remote(array, array, twin_send.at[a, part], twin_recv.at[a, part], twin)
 
     def pair_copy(a, way):
         at = block(z)
@@ -291,24 +315,31 @@
             full.at[a, way, at, :], other.at[a, way, at, :], pair_send.at[a, way], pair_recv.at[a, way], pair
         )
 
-    for way in (0, 1):
+    for part in (0, 1):
         value = []
         for a in (GATE, UP, ACT):
-            swap_copy(a, way).wait_recv()
-            value.append(own[a, way] + swap_in[a, way].astype(jnp.float32))
+            swap_copy(a, part).wait_recv()
+            value.append(own[a, part, lot(h), :] + swap_in[a, part].astype(jnp.float32))
         gate_pre, up_pre, grad_act = value
         sigmoid_gate = jax.nn.sigmoid(gate_pre)
         gated = gate_pre * sigmoid_gate
-        full[ACT, way, block(z), :] = (gated * up_pre).astype(jnp.bfloat16)
-        gather_start(ACT, way)
-        full[GATE, way, block(z), :] = (
+        full[ACT, part, piece(z, 0), :] = (gated * up_pre).astype(jnp.bfloat16)
+        twin_copy(ACT, part).start()
+        gather_start(ACT, part, 0)
+        full[GATE, part, piece(z, 0), :] = (
             grad_act * up_pre * sigmoid_gate * (1.0 + gate_pre * (1.0 - sigmoid_gate))
         ).astype(jnp.bfloat16)
-        gather_start(GATE, way)
-        full[UP, way, block(z), :] = (grad_act * gated).astype(jnp.bfloat16)
-    for way in (0, 1):
-        pair_copy(GATE, way).start()
-        pair_copy(UP, way).start()
+        twin_copy(GATE, part).start()
+        gather_start(GATE, part, 0)
+        full[UP, part, piece(z, 0), :] = (grad_act * gated).astype(jnp.bfloat16)
+        twin_copy(UP, part).start()
+        gather_start(UP, part, 0)
+    for a in (ACT, GATE):
+        for part in (0, 1):
+            twin_copy(a, part).wait_recv()
+            gather_start(a, part, 1)
+            if a != ACT:
+                pair_copy(a, part).start()
     x_copy = remote(x_ref, x_other, x_send, x_recv, pair)
     x_copy.start()
     x_turned[...] = x_ref[...].T
@@ -326,7 +357,9 @@
     gather_step(ACT, 0)
     gather_step(GATE, 0)
     for part in (0, 1):
-        gather_start(UP, part)
+        twin_copy(UP, part).wait_recv()
+        gather_start(UP, part, 1)
+        pair_copy(UP, part).start()
     gather_step(ACT, 1)
     gather_step(GATE, 1)
     gather_step(UP, 0)
@@ -336,7 +369,8 @@
     for a in (GATE, UP):
         for part in (0, 1):
             pair_copy(a, part).wait_recv()
-            gather_start(OTHER + a, part)
+            for which in (0, 1):
+                gather_start(OTHER + a, part, which)
     down_part(0)
     gather_step(UP, 2)
     down_part(1)
@@ -398,12 +432,13 @@
     mine = jnp.sum(jnp.where(d_line == d, expert_ref[...], 0), axis=1, keepdims=True)
     theirs = jnp.sum(jnp.where(d_line == pair[1], expert_ref[...], 0), axis=1, keepdims=True)
     shared = jnp.where(mine == theirs, 1.0, 0.0)
-    for a, out in ((GATE, grad_gate_ref), (UP, grad_up_ref)):
+    def finish(a, out):
         for way in (0, 1):
             gather_end(OTHER + a, way)
             part = part_own[a, way] + shared * contract(x_turned[...], other[a, way], 1, 0)
             out[:, pl.ds(way * half, half)] = part.astype(jnp.bfloat16)
 
+    finish(GATE, grad_gate_ref)
     everything_back = remote(
         back.at[pl.ds(0, near - 1)], back.at[pl.ds(0, near - 1)], back_near_send, back_near_recv, near_peer(1)
     )
@@ -418,6 +453,8 @@
         grad_down_ref[at, :] = (
             grad_down_ref[at, :].astype(jnp.float32) + shared * down_in[way].astype(jnp.float32)
         ).astype(jnp.bfloat16)
+
+    finish(UP, grad_up_ref)
 
     near_all.wait_send()
     everything_back.wait_send()
@@ -431,22 +468,19 @@
         for a in (GATE, UP):
             pair_copy(a, way).wait_send()
 
-    def drain(part, carry):
-        for way in (0, 1):
-            for a in range(5):
-                for step in range(reach - 1):
-                    gather_copy(a, way, part, step).wait_send()
-            for a in (GATE, UP, ACT):
+    for part in (0, 1):
+        for a in (GATE, UP, ACT):
+            twin_copy(a, part).wait_send()
+            ring_copy(a, part, part, 0).wait_send()
+            for way in (0, 1):
                 for step in range(1, reach):
                     ring_copy(a, way, part, step).wait_send()
         for a in range(5):
-            gather_copy(a, part, part, reach - 1).wait_send()
-        for a in (GATE, UP, ACT):
-            ring_copy(a, part, part, 0).wait_send()
-        return carry
-
-    for part in (0, 1):
-        drain(part, 0)
+            for which in (0, 1):
+                gather_copy(a, part, part, reach - 1, which).wait_send()
+                for way in (0, 1):
+                    for step in range(reach - 1):
+                        gather_copy(a, way, part, step, which).wait_send()
 
 
 def slot_call(routes, prob, grad_out, expert, x, gate_w, up_w, down_w):
@@ -489,7 +523,7 @@
             pltpu.VMEM((3, 2, 2, nz // 2 + 1, part, half), bf16),
             pltpu.VMEM((3, 2, part, half), f32),
             pltpu.VMEM((3, 2, part, half), bf16),
-            pltpu.VMEM((3, 2, part, half), bf16),
+            pltpu.VMEM((3, 2, part // 2, half), bf16),
             pltpu.VMEM((3, 2, count, half), bf16),
             pltpu.VMEM((2, 2, count, half), bf16),
             pltpu.VMEM((count, width), bf16),
@@ -511,8 +545,10 @@
             dma((3, 2, 2, nz // 2)),
             dma((3, 2)),
             dma((3, 2)),
-            dma((5, 2, 2, nz // 2)),
-            dma((5, 2, 2, nz // 2)),
+            dma((3, 2)),
+            dma((3, 2)),
+            dma((5, 2, 2, 2, nz // 2)),
+            dma((5, 2, 2, 2, nz // 2)),
             dma((2, 2)),
             dma((2, 2)),
             dma,

time: 138 us -> 143 us (1.036)
  Pallas kernels: 132 us -> 137 us
    pallas_call x1, Pallas kernels: 132 us -> 137 us  [slot_call(): pl.pallas_call(slot_kernel, out_shape=(jax.ShapeDtypeStruct((tokens, widt...]
where the time goes in v4:
time: 143 us; the launch traced here: 142 us
  Pallas kernels  137 us (96%)
  local copies, waits for them, and re-layouts  5.28 us (4%)
    pallas_call x1, Pallas kernels, slot_call(): pl.pallas_call(slot_kernel, out_shape=(jax.ShapeDtypeStruct((tokens, widt...  137 us
    unnamed x8, local copies, waits for them, and re-layouts  5.28 us

profile of v4, /device:TPU:1, one launch (start us, length us, event | category | flops | bytes accessed | tf_op | source)
XLA Modules:
  0.0 142.5 jit_solution(13042046398395682486)
XLA Ops:
  0.6 136.6 %shard_map.111 = (bf16[32,256]{1,0:T(8,128)(2,1)}, bf16[256,1024]{1,0:T(8,128)(2,1)}, bf16[256,1024]{1,0:T(8,128)(2,1)}, bf16[1024,256]{1,0:T(8,128)(2,1)}) custom-call(s32[8,32]{1,0:T(8,128)} %bitcast.17, f32[8,32]{1,0:T(8,128)} %bitcast.18, bf16[32,256]{1,0:T(8,128)(2,1)} %grad_out_ref.1, s32[1,64]{1,0:T(1,128)} %bitcast.19, bf16[512,256]{1,0:T(8,128)(2,1)} %bitcast.16, ...), custom_call_target="tpu_custom_call" | custom-call | tf_op jit(solution)/shard_map/pallas_call | solution.py:500
  137.2 1.3 copy.16
  138.5 0.0 copy-start.1
  138.5 1.9 %copy.17 = bf16[1,256,1024]{2,1,0:T(8,128)(2,1)} copy(bf16[1,256,1024]{2,1,0:T(8,128)(2,1)} %bitcast.12) | data formatting | bytes 1048576
  140.4 0.0 copy-done.1
  140.4 0.0 copy-start
  140.5 0.8 copy.18
  141.2 0.4 copy-done
  141.7 0.8 copy.19
Async XLA Ops:
  138.5 1.9 %copy-start.1 = (bf16[256,1024]{1,0:T(8,128)(2,1)S(1)}, bf16[256,1024]{1,0:T(8,128)(2,1)}, u32[]{:S(2)}) copy-start(bf16[256,1024]{1,0:T(8,128)(2,1)} %get-tuple-element.10) | copy-start | bytes 1572868
  140.4 1.2 copy-start
